TPU v7x, 32 devices: a whole 2x2x4 slice. The times are simulated.
32 devices in a mesh: row: 16 (over z, y, x), col: 2 (over core).
Axes of the slice: x: 2, y: 2, z: 4, core: 2. Of those that a mesh axis runs over, the one named last changes fastest.
Arguments:
- embeddings: bfloat16 [16384, 2048], P(('row', 'col')), may hold values from -6 to 6
- inverse_scales: float32 [2048], replicated, may hold values from 0.0039774757 to 0.059662133
- matches: int32 [16384, 2], replicated, may hold values from 0 to 16383
Outputs:
- trailing: float32 [16384, 4096], P('row', 'col')
- factor: float32 [16384, 1024], P(('row', 'col'))
Inputs may be any that keep to these rules, and one draw needn't show every extreme that they name: `matches`: candidate indices of the winner and the loser of each match.
All inputs are finite; a program needn't handle non-finite values.
Results may differ from a plain program's by a relative error of at most 0.0065.
Values may be sent and summed in bfloat16 or wider, within the bound.
No kernel may reach another device: no remote copies, remote signals or barrier semaphores. Data moves between devices by JAX's collectives and lax.ppermute only.
A program may use at most 128 MiB of HBM per device.

v0:
```python
import math

import jax
import jax.numpy as jnp
from jax import lax
from jax.sharding import PartitionSpec as P

PANEL = 1024
STOPS = 4


def passed_along(block, axis, distance):
    devices = range(lax.axis_size(axis))
    route = [((i - distance) % len(devices), i) for i in devices]
    return lax.ppermute(block, axis, route)


def squares_of(scaled):
    values = scaled.astype(jnp.float32)
    return jnp.sum(values * values, axis=1)


def kernel_block(left, left_sq, right, right_sq):
    inner = jnp.dot(left, right.T, preferred_element_type=jnp.float32)
    return jnp.exp(-0.5 * (left_sq[:, None] + right_sq[None, :] - 2.0 * inner))


def match_counts(identity, matches):
    total = matches.shape[0]
    group_rows = math.gcd(total, 1024)
    grouped = matches.reshape(total // group_rows, group_rows, 2)

    def accumulate(carry, group):
        hits = (group[:, 0:1] == identity[None, :]).astype(jnp.float32)
        hits = hits + (group[:, 1:2] == identity[None, :]).astype(jnp.float32)
        return (carry + jnp.sum(hits, axis=0), None)

    counts, unused = lax.scan(accumulate, jnp.zeros(identity.shape, jnp.float32), grouped)
    return 0.1 + 0.5 * counts


def with_extras(block, row_ids, column_ids, row_extra):
    return block + jnp.where(row_ids[:, None] == column_ids[None, :], row_extra[:, None], 0.0)


def solve_rows(lower, rows):
    return lax.linalg.triangular_solve(lower, rows, left_side=False, lower=True, transpose_a=True)


def body(embeddings, inverse_scales, matches):
    row_count = lax.axis_size("row")
    col_count = lax.axis_size("col")
    row_index = lax.axis_index("row")
    col_index = lax.axis_index("col")
    slice_rows = embeddings.shape[0]
    block_rows = slice_rows * col_count
    panel_share = PANEL // row_count
    scaled = (embeddings.astype(jnp.float32) * inverse_scales[None, :]).astype(jnp.bfloat16)
    own_sq = squares_of(scaled)
    own_ids = (
        row_index * block_rows + col_index * slice_rows + jnp.arange(slice_rows, dtype=jnp.int32)
    )
    own_extra = match_counts(own_ids, matches)
    block_scaled = lax.all_gather(scaled, "col", axis=0, tiled=True)
    block_sq = squares_of(block_scaled)
    lead_scaled = block_scaled[:panel_share]
    panel_scaled = lax.all_gather(lead_scaled, "row", axis=0, tiled=True)
    panel_sq = squares_of(panel_scaled)
    panel_ids = (
        jnp.arange(row_count, dtype=jnp.int32)[:, None] * block_rows
        + jnp.arange(panel_share, dtype=jnp.int32)[None, :]
    ).reshape(-1)
    lead_ids = row_index * block_rows + jnp.arange(panel_share, dtype=jnp.int32)
    leading = with_extras(
        kernel_block(lead_scaled, block_sq[:panel_share], panel_scaled, panel_sq),
        lead_ids,
        panel_ids,
        match_counts(lead_ids, matches),
    )
    diagonal = lax.all_gather(leading, "row", axis=0, tiled=True)
    lower = jnp.linalg.cholesky(diagonal)
    own_rows = with_extras(
        kernel_block(scaled, own_sq, panel_scaled, panel_sq), own_ids, panel_ids, own_extra
    )
    own_factor = solve_rows(lower, own_rows)
    block_factor = lax.all_gather(own_factor, "col", axis=0, tiled=True)

    def stop_tile(visit_scaled, visit_factor):
        tile = kernel_block(block_scaled, block_sq, visit_scaled, squares_of(visit_scaled))
        return tile - jnp.dot(block_factor, visit_factor.T, precision=lax.Precision.HIGHEST)

    local_cols = col_index * slice_rows + jnp.arange(slice_rows, dtype=jnp.int32)
    first = stop_tile(scaled, own_factor)
    first = first + jnp.where(
        jnp.arange(block_rows, dtype=jnp.int32)[:, None] == local_cols[None, :],
        own_extra[None, :],
        0.0,
    )
    pieces = [first]
    visitor = (scaled, own_factor)
    for stop in range(1, STOPS):
        visitor = (
            passed_along(visitor[0].astype(jnp.float32), "row", 1).astype(jnp.bfloat16),
            passed_along(visitor[1], "row", 1),
        )
        pieces.append(stop_tile(visitor[0], visitor[1]))
    trailing = jnp.concatenate(pieces, axis=1)
    return (trailing, own_factor)


def solution(mesh):
    return jax.shard_map(
        body,
        mesh=mesh,
        in_specs=(P(("row", "col"), None), P(), P()),
        out_specs=(P("row", "col"), P(("row", "col"), None)),
        check_vma=False,
    )
```

profile of v0, /device:TPU:0, one launch (start us, length us, event | category | flops | bytes accessed | tf_op | source)
XLA Modules:
  0.0 798.4 jit_solution(4340165628868113637)
XLA Ops:
  7.2 3.6 multiply_reduce_fusion.5
  12.4 2.9 collective-permute-start
  15.5 11.9 %all-gather.5.cloned.1.call-done = bf16[1024,2048]{1,0:T(8,128)(2,1)} async-done(((bf16[512,2048]{1,0:T(8,128)(2,1)}), bf16[1024,2048]{1,0:T(8,128)(2,1)}) %all-gather.5.cloned.1.call-update) | async-done | bytes 4194320 | tf_op jit(solution)/shard_map/all_gather | solution.py:64
  29.1 15.5 %while.25 = (s32[]{:T(128)}, f32[64]{0:T(128)S(1)}, s32[16,1024,2]{1,2,0:T(2,128)}, s32[]{:T(128)}, s32[]{:T(128)}, /*index=5*/s32[]{:T(128)}) while((s32[]{:T(128)}, f32[64]{0:T(128)S(1)}, s32[16,1024,2]{1,2,0:T(2,128)}, s32[]{:T(128)}, s32[]{:T(128)}, /*index=5*/s32[]{:T(128)}) %tuple.122), condition=%wide.region_8.9_spmd.clone, body=%wide.region_6.8_spmd.clone.sunk | while | flops 393347 | bytes 42583 | solution.py:38
  44.6 3.1 multiply_reduce_fusion.1
  47.7 74.6 %all-gather.7.cloned.1.call-done = bf16[1024,2048]{1,0:T(8,128)(2,1)} async-done(((bf16[64,2048]{1,0:T(8,128)(2,1)}), bf16[1024,2048]{1,0:T(8,128)(2,1)}) %all-gather.7.cloned.1.call-update) | async-done | bytes 4194320 | tf_op jit(solution)/shard_map/all_gather | solution.py:67
  122.3 3.2 multiply_reduce_fusion
  125.8 3.1 fusion.9
  128.9 22.5 %while.24 = (s32[]{:T(128)}, f32[512]{0:T(512)S(1)}, s32[16,1024,2]{1,2,0:T(2,128)}, s32[]{:T(128)}, s32[]{:T(128)}, /*index=5*/s32[]{:T(128)}) while((s32[]{:T(128)}, f32[512]{0:T(512)S(1)}, s32[16,1024,2]{1,2,0:T(2,128)}, s32[]{:T(128)}, s32[]{:T(128)}, /*index=5*/s32[]{:T(128)}) %tuple.123), condition=%wide.region_5.6_spmd.clone, body=%wide.region_3.0_spmd.clone.sunk | while | flops 3146755 | bytes 53335 | solution.py:38
  153.0 6.4 select_add_fusion.2
  159.4 71.4 %all-gather.9.cloned.1.call-done = f32[1024,1024]{1,0:T(8,128)} async-done(((f32[64,1024]{1,0:T(8,128)}), f32[1024,1024]{1,0:T(8,128)}) %all-gather.9.cloned.1.call-update) | async-done | bytes 4194320 | tf_op jit(solution)/shard_map/all_gather | solution.py:80
  230.8 5.8 copy.12
  236.6 4.4 fusion.5
  243.0 11.7 %cholesky.223 = f32[128,128]{1,0:T(8,128)S(1)} custom-call(f32[128,128]{1,0:T(8,128)S(1)} %cholesky.580), custom_call_target="Cholesky" | custom-call | tf_op jit(solution)/shard_map/jit(cholesky)/cholesky | solution.py:81
  254.8 9.8 %custom-call.62 = f32[1,128,128]{1,2,0:T(8,128)S(1)} custom-call(f32[1,128,128]{2,1,0:T(8,128)S(1)} %get-tuple-element.176), custom_call_target="InvertDiagBlocksLowerTriangular" | custom-call | tf_op jit(solution)/shard_map/jit(cholesky)/cholesky | solution.py:81
  271.0 11.9 %cholesky.244 = f32[128,128]{1,0:T(8,128)S(1)} custom-call(f32[128,128]{1,0:T(8,128)S(1)} %cholesky.584), custom_call_target="Cholesky" | custom-call | tf_op jit(solution)/shard_map/jit(cholesky)/cholesky | solution.py:81
  283.5 9.8 %custom-call.63 = f32[1,128,128]{1,2,0:T(8,128)S(1)} custom-call(f32[1,128,128]{2,1,0:T(8,128)S(1)} %get-tuple-element.173), custom_call_target="InvertDiagBlocksLowerTriangular" | custom-call | tf_op jit(solution)/shard_map/jit(cholesky)/cholesky | solution.py:81
  296.6 11.7 %cholesky.468 = f32[128,128]{1,0:T(8,128)S(1)} custom-call(f32[128,128]{1,0:T(8,128)S(1)} %cholesky.589), custom_call_target="Cholesky" | custom-call | tf_op jit(solution)/shard_map/jit(cholesky)/cholesky | solution.py:81
  309.6 9.8 %custom-call.64 = f32[1,128,128]{1,2,0:T(8,128)S(1)} custom-call(f32[1,128,128]{2,1,0:T(8,128)S(1)} %get-tuple-element.170), custom_call_target="InvertDiagBlocksLowerTriangular" | custom-call | tf_op jit(solution)/shard_map/jit(cholesky)/cholesky | solution.py:81
  322.9 11.9 %cholesky.487 = f32[128,128]{1,0:T(8,128)S(1)} custom-call(f32[128,128]{1,0:T(8,128)S(1)} %cholesky.594), custom_call_target="Cholesky" | custom-call | tf_op jit(solution)/shard_map/jit(cholesky)/cholesky | solution.py:81
  336.1 9.8 %custom-call.65 = f32[1,128,128]{1,2,0:T(8,128)S(1)} custom-call(f32[1,128,128]{2,1,0:T(8,128)S(1)} %get-tuple-element.167), custom_call_target="InvertDiagBlocksLowerTriangular" | custom-call | tf_op jit(solution)/shard_map/jit(cholesky)/cholesky | solution.py:81
  349.3 11.7 %cholesky.506 = f32[128,128]{1,0:T(8,128)S(1)} custom-call(f32[128,128]{1,0:T(8,128)S(1)} %cholesky.599), custom_call_target="Cholesky" | custom-call | tf_op jit(solution)/shard_map/jit(cholesky)/cholesky | solution.py:81
  362.3 10.2 %custom-call.66 = f32[1,128,128]{1,2,0:T(8,128)S(1)} custom-call(f32[1,128,128]{2,1,0:T(8,128)S(1)} %get-tuple-element.164), custom_call_target="InvertDiagBlocksLowerTriangular" | custom-call | tf_op jit(solution)/shard_map/jit(cholesky)/cholesky | solution.py:81
  375.9 11.7 %cholesky.526 = f32[128,128]{1,0:T(8,128)S(1)} custom-call(f32[128,128]{1,0:T(8,128)S(1)} %cholesky.604), custom_call_target="Cholesky" | custom-call | tf_op jit(solution)/shard_map/jit(cholesky)/cholesky | solution.py:81
  388.9 9.8 %custom-call.67 = f32[1,128,128]{1,2,0:T(8,128)S(1)} custom-call(f32[1,128,128]{2,1,0:T(8,128)S(1)} %get-tuple-element.161), custom_call_target="InvertDiagBlocksLowerTriangular" | custom-call | tf_op jit(solution)/shard_map/jit(cholesky)/cholesky | solution.py:81
  401.7 11.9 %cholesky.546 = f32[128,128]{1,0:T(8,128)S(1)} custom-call(f32[128,128]{1,0:T(8,128)S(1)} %cholesky.609), custom_call_target="Cholesky" | custom-call | tf_op jit(solution)/shard_map/jit(cholesky)/cholesky | solution.py:81
  414.8 9.8 %custom-call.68 = f32[1,128,128]{1,2,0:T(8,128)S(1)} custom-call(f32[1,128,128]{2,1,0:T(8,128)S(1)} %get-tuple-element.158), custom_call_target="InvertDiagBlocksLowerTriangular" | custom-call | tf_op jit(solution)/shard_map/jit(cholesky)/cholesky | solution.py:81
  427.2 11.7 %cholesky.564 = f32[128,128]{1,0:T(8,128)S(1)} custom-call(f32[128,128]{1,0:T(8,128)S(1)} %convolution_subtract_fusion.13), custom_call_target="Cholesky" | custom-call | tf_op jit(solution)/shard_map/jit(cholesky)/cholesky | solution.py:81
  445.8 4.9 select_select_fusion
  450.7 22.8 %while.23 = (s32[]{:T(128)}, f32[1024,1024]{1,0:T(8,128)}, s32[8,2]{0,1:T(2,128)S(1)}, f32[8,128,128]{2,1,0:T(8,128)S(1)}, s32[]{:T(128)}) while((s32[]{:T(128)}, f32[1024,1024]{1,0:T(8,128)}, s32[8,2]{0,1:T(2,128)S(1)}, f32[8,128,128]{2,1,0:T(8,128)S(1)}, s32[]{:T(128)}) %tuple.108), condition=%wide.while_cond, body=%wide.while_body.sunk | while | flops 2 | bytes 131181 | solution.py:47
  473.6 79.0 %custom-call.69 = f32[8,128,128]{1,2,0:T(8,128)S(1)} custom-call(f32[8,128,128]{2,1,0:T(8,128)S(1)} %get-tuple-element.55), custom_call_target="InvertDiagBlocksLowerTriangular" | custom-call | tf_op jit(solution)/shard_map/triangular_solve | solution.py:47
  564.8 3.2 convolution_subtract_fusion.4
  568.5 3.6 convolution_subtract_fusion.7
  572.6 4.3 convolution_subtract_fusion.3
  584.0 45.5 %collective-permute-done.1 = f32[512,1024]{0,1:T(8,128)} collective-permute-done((f32[512,1024]{0,1:T(8,128)S(1)}, f32[512,1024]{0,1:T(8,128)}, u32[]{:S(2)}, u32[]{:S(2)}) %collective-permute-start.1) | collective-permute-done | bytes 2097184 | tf_op jit(solution)/shard_map/ppermute | solution.py:15
  629.6 5.3 fusion.83
  634.9 5.3 fusion.82
  640.2 34.2 %collective-permute-done.4 = bf16[512,2048]{1,0:T(8,128)(2,1)S(1)} collective-permute-done((bf16[512,2048]{1,0:T(8,128)(2,1)}, bf16[512,2048]{1,0:T(8,128)(2,1)S(1)}, u32[]{:S(2)}, u32[]{:S(2)}) %collective-permute-start.4) | collective-permute-done | bytes 2097184 | tf_op jit(solution)/shard_map/ppermute | solution.py:15
  674.9 3.7 fusion.81
  680.4 38.5 %collective-permute-done.3 = f32[512,1024]{0,1:T(8,128)} collective-permute-done((f32[512,1024]{0,1:T(8,128)}, f32[512,1024]{0,1:T(8,128)}, u32[]{:S(2)}, u32[]{:S(2)}) %collective-permute-start.3) | collective-permute-done | bytes 2097184 | tf_op jit(solution)/shard_map/ppermute | solution.py:15
  718.9 9.5 %fusion.80 = f32[1024,512]{0,1:T(8,128)S(1)} fusion(f32[1024,1024]{0,1:T(8,128)} %all-gather.11.cloned.1.call-done, f32[512,1024]{0,1:T(8,128)S(1)} %copy-done.2), kind=kOutput, calls=%fused_computation.203 | convolution fusion | flops 6442450944 | bytes 8388608 | tf_op jit(solution)/shard_map/dot_general | solution.py:90
  728.4 8.9 %exponential_subtract_fusion.2 = f32[1024,512]{0,1:T(8,128)S(1)} fusion(f32[1024,512]{0,1:T(8,128)S(1)} %copy-done.11, f32[1024,1024]{0,1:T(8,128)S(1)} %copy-done, f32[512,1024]{0,1:T(8,128)} %collective-permute-done.1, f32[512]{0:T(512)S(1)} %multiply_reduce_fusion.4, f32[1024]{0:T(1024)S(1)} %multiply_reduce_fusion.1), kind=kOutput, calls=%fused_computation.27 | convolution fusion | flops 6445072384 | bytes 10491904 | tf_op jit(solution)/shard_map/dot_general | solution.py:90
  737.4 9.1 %exponential_subtract_fusion.1 = f32[1024,512]{0,1:T(8,128)S(1)} fusion(f32[1024,512]{0,1:T(8,128)S(1)} %copy-done.10, f32[1024,1024]{0,1:T(8,128)S(1)} %copy-done, f32[512,1024]{0,1:T(8,128)} %collective-permute-done.3, f32[512]{0:T(512)S(1)} %multiply_reduce_fusion.3, f32[1024]{0:T(1024)S(1)} %multiply_reduce_fusion.1), kind=kOutput, calls=%fused_computation.26 | convolution fusion | flops 6445072384 | bytes 10491904 | tf_op jit(solution)/shard_map/dot_general | solution.py:90
  746.5 2.9 select_add_fusion.1
  749.3 20.5 %collective-permute-done.5 = f32[512,1024]{0,1:T(8,128)} collective-permute-done((f32[512,1024]{0,1:T(8,128)}, f32[512,1024]{0,1:T(8,128)}, u32[]{:S(2)}, u32[]{:S(2)}) %collective-permute-start.5) | collective-permute-done | bytes 2097184 | tf_op jit(solution)/shard_map/ppermute | solution.py:15
  769.9 8.7 %exponential_subtract_fusion = f32[1024,512]{0,1:T(8,128)S(1)} fusion(f32[1024,512]{0,1:T(8,128)S(1)} %copy-done.9, f32[1024,1024]{0,1:T(8,128)S(1)} %copy-done, f32[512,1024]{0,1:T(8,128)} %collective-permute-done.5, f32[512]{0:T(512)S(1)} %multiply_reduce_fusion.2, f32[1024]{0:T(1024)S(1)} %multiply_reduce_fusion.1), kind=kOutput, calls=%fused_computation.25 | convolution fusion | flops 6445072384 | bytes 10491904 | tf_op jit(solution)/shard_map/dot_general | solution.py:90
  778.6 4.0 pad_maximum_fusion
  782.6 9.1 %copy.13 = f32[1024,2048]{1,0:T(8,128)} copy(f32[1024,2048]{0,1:T(8,128)} %pad_maximum_fusion) | data formatting | bytes 16777216
  (294 shorter events, 124.3 us)
Async XLA Ops:
  7.2 20.2 %all-gather.5.cloned.1.call-start = ((), (), s32[]{:S(2)}) async-start(), calls=%async_computation | async-start | bytes 6291456 | tf_op jit(solution)/shard_map/all_gather | solution.py:64
  10.8 1.6 copy-start.5
  10.8 111.5 %all-gather.7.cloned.1.call-start = ((), (), s32[]{:S(2)}) async-start(), calls=%async_computation.1 | async-start | bytes 4456448 | tf_op jit(solution)/shard_map/all_gather | solution.py:67
  12.4 139.1 %collective-permute-start = (bf16[512,2048]{1,0:T(8,128)(2,1)S(1)}, bf16[512,2048]{1,0:T(8,128)(2,1)}, u32[]{:S(2)}, u32[]{:S(2)}) collective-permute-start(bf16[512,2048]{1,0:T(8,128)(2,1)S(1)} %copy-done.5), channel_id=1, source_target_pairs={{30,0},{0,2},{2,4},{4,6},{6,8},{8,10},{10,12},{12,14},{14,16},{16,... | collective-permute-start | bytes 6291464 | tf_op jit(solution)/shard_map/ppermute | solution.py:15
  29.0 201.8 %all-gather.9.cloned.1.call-start = ((), (), s32[]{:S(2)}) async-start(), calls=%async_computation.2 | async-start | bytes 4456448 | tf_op jit(solution)/shard_map/all_gather | solution.py:80
  122.3 3.4 copy-start.3
  128.9 590.0 %all-gather.11.cloned.1.call-start = ((), (), s32[]{:S(2)}) async-start(), calls=%async_computation.3 | async-start | bytes 6291456 | tf_op jit(solution)/shard_map/all_gather | solution.py:86
  151.5 427.0 %collective-permute-start.2 = (bf16[512,2048]{1,0:T(8,128)(2,1)}, bf16[512,2048]{1,0:T(8,128)(2,1)}, u32[]{:S(2)}, u32[]{:S(2)}) collective-permute-start(bf16[512,2048]{1,0:T(8,128)(2,1)} %collective-permute-done), channel_id=1, source_target_pairs={{30,0},{0,2},{2,4},{4,6},{6,8},{8,10},{10,12},{12,14},{14,16},{16,... | collective-permute-start | bytes 6291464 | tf_op jit(solution)/shard_map/ppermute | solution.py:15
  241.1 2.0 copy-start.4
  555.6 3.1 copy-start.12
  577.2 1.3 copy-start.1
  577.2 52.3 %collective-permute-start.1 = (f32[512,1024]{0,1:T(8,128)S(1)}, f32[512,1024]{0,1:T(8,128)}, u32[]{:S(2)}, u32[]{:S(2)}) collective-permute-start(f32[512,1024]{0,1:T(8,128)S(1)} %convolution_dynamic-update-slice_fusion.2), channel_id=1, source_target_pairs={{30,0},{0,2},{2,4},{4,6},{6,8},{8,10},{10,12},{12,14},{14,16},{16,... | collective-permute-start | bytes 6291464 | tf_op jit(solution)/shard_map/ppermute | solution.py:15
  578.6 95.8 %collective-permute-start.4 = (bf16[512,2048]{1,0:T(8,128)(2,1)}, bf16[512,2048]{1,0:T(8,128)(2,1)S(1)}, u32[]{:S(2)}, u32[]{:S(2)}) collective-permute-start(bf16[512,2048]{1,0:T(8,128)(2,1)} %collective-permute-done.2), channel_id=1, source_target_pairs={{30,0},{0,2},{2,4},{4,6},{6,8},{8,10},{10,12},{12,14},{14,16},{16,... | collective-permute-start | bytes 6291464 | tf_op jit(solution)/shard_map/ppermute | solution.py:15
  579.7 49.9 %copy-start.7 = (bf16[1024,2048]{1,0:T(8,128)(2,1)S(1)}, bf16[1024,2048]{1,0:T(8,128)(2,1)}, u32[]{:S(2)}) copy-start(bf16[1024,2048]{1,0:T(8,128)(2,1)} %all-gather.5.cloned.1.call-done) | copy-start | bytes 12582916
  629.6 89.3 %collective-permute-start.3 = (f32[512,1024]{0,1:T(8,128)}, f32[512,1024]{0,1:T(8,128)}, u32[]{:S(2)}, u32[]{:S(2)}) collective-permute-start(f32[512,1024]{0,1:T(8,128)} %collective-permute-done.1), channel_id=1, source_target_pairs={{30,0},{0,2},{2,4},{4,6},{6,8},{8,10},{10,12},{12,14},{14,16},{16,... | collective-permute-start | bytes 6291464 | tf_op jit(solution)/shard_map/ppermute | solution.py:15
  674.9 3.7 copy-start.2
  718.9 51.0 %collective-permute-start.5 = (f32[512,1024]{0,1:T(8,128)}, f32[512,1024]{0,1:T(8,128)}, u32[]{:S(2)}, u32[]{:S(2)}) collective-permute-start(f32[512,1024]{0,1:T(8,128)} %collective-permute-done.3), channel_id=1, source_target_pairs={{30,0},{0,2},{2,4},{4,6},{6,8},{8,10},{10,12},{12,14},{14,16},{16,... | collective-permute-start | bytes 6291464 | tf_op jit(solution)/shard_map/ppermute | solution.py:15
  718.9 9.5 %copy-start = (f32[1024,1024]{0,1:T(8,128)S(1)}, f32[1024,1024]{0,1:T(8,128)}, u32[]{:S(2)}) copy-start(f32[1024,1024]{0,1:T(8,128)} %all-gather.11.cloned.1.call-done) | copy-start | bytes 12582916
  718.9 9.5 %copy-start.11 = (f32[1024,512]{0,1:T(8,128)S(1)}, f32[1024,512]{0,1:T(8,128)}, u32[]{:S(2)}) copy-start(f32[1024,512]{0,1:T(8,128)} %fusion.83) | copy-start | bytes 6291460
  728.4 8.9 %copy-start.10 = (f32[1024,512]{0,1:T(8,128)S(1)}, f32[1024,512]{0,1:T(8,128)}, u32[]{:S(2)}) copy-start(f32[1024,512]{0,1:T(8,128)} %fusion.82) | copy-start | bytes 6291460
  737.3 9.1 %copy-start.6 = (bf16[512,2048]{1,0:T(8,128)(2,1)S(1)}, bf16[512,2048]{1,0:T(8,128)(2,1)}, u32[]{:S(2)}) copy-start(bf16[512,2048]{1,0:T(8,128)(2,1)} %get-tuple-element.123) | copy-start | bytes 6291460
  737.3 9.1 %copy-start.8 = (bf16[1024,2048]{1,0:T(8,128)(2,1)S(1)}, bf16[1024,2048]{1,0:T(8,128)(2,1)}, u32[]{:S(2)}) copy-start(bf16[1024,2048]{1,0:T(8,128)(2,1)} %all-gather.5.cloned.1.call-done) | copy-start | bytes 12582916
  746.4 23.4 %copy-start.9 = (f32[1024,512]{0,1:T(8,128)S(1)}, f32[1024,512]{0,1:T(8,128)}, u32[]{:S(2)}) copy-start(f32[1024,512]{0,1:T(8,128)} %fusion.81) | copy-start | bytes 6291460
Sparse Core Ops, SparseCore 0:
  10.9 16.3 all-gather.4
  30.7 91.5 all-gather.6
  129.0 101.8 all-gather.8
  578.7 15.3 all-gather.10
where the time goes:
time: 807 us; the launch traced here: 798 us
  waiting for transfers between devices  297 us (37%)
  other arithmetic  294 us (36%)
  matrix products  110 us (14%)
  local copies, waits for them, and re-layouts  71.5 us (9%)
  between operations  19.4 us (2%)
    another operation x30, other arithmetic, body(): lower = jnp.linalg.cholesky(diagonal)  172 us
    ppermute x6, waiting for transfers between devices, passed_along(): return lax.ppermute(block, axis, route)  139 us
    another operation x3, other arithmetic, solve_rows(): lax.linalg.triangular_solve(lower, rows, left_side=False, lower=True, tra...  83.9 us
    all_gather x1, waiting for transfers between devices, body(): panel_scaled = lax.all_gather(lead_scaled, 'row', axis=0, tiled=True)  74.6 us
    all_gather x1, waiting for transfers between devices, body(): diagonal = lax.all_gather(leading, 'row', axis=0, tiled=True)  71.4 us
    dot_general x4, matrix products, stop_tile(): jnp.dot(block_factor, visit_factor.T, precision=lax.Precision.HIGHEST)  36.2 us
    dot_general x6, matrix products, kernel_block(): inner = jnp.dot(left, right.T, preferred_element_type=jnp.float32)  26.7 us
    another operation x15, matrix products, solve_rows(): lax.linalg.triangular_solve(lower, rows, left_side=False, lower=True, tra...  24.5 us
  transfers between devices with their start and end apart: 10, of which 7 were waited for; matrix products, arithmetic and copies ran while one was open for 56% of the time, Pallas kernels for 0%

commit v1 on v0

v1 whole, which is shorter than its diff:
```python
import functools

import jax
import jax.numpy as jnp
from jax import lax
from jax.experimental import pallas as pl
from jax.experimental.pallas import tpu as pltpu
from jax.sharding import PartitionSpec as P

PANEL = 1024
STOPS = 4
LAYER = 4
BLOCK = 128
GROUP = 8
BAND = 32
CHUNK = 256
VMEM_BYTES = 56 * 1024 * 1024

F32 = jnp.float32
BF16 = jnp.bfloat16
NT = (((1,), (1,)), ((), ()))
NN = (((1,), (0,)), ((), ()))


def rotated(block, axis, distance):
    count = lax.axis_size(axis)
    return lax.ppermute(block, axis, [(i, (i + distance) % count) for i in range(count)])


def split(values):
    high = values.astype(BF16)
    low = (values - high.astype(F32)).astype(BF16)
    return high, low


def dot(left, right, dims):
    return lax.dot_general(left, right, dims, preferred_element_type=F32)


def dot3(left, right, dims):
    (lh, ll), (rh, rl) = left, right
    return dot(lh, rh, dims) + (dot(lh, rl, dims) + dot(ll, rh, dims))


def half_squares(block):
    values = block.astype(F32)
    return 0.5 * jnp.sum(values * values, axis=1, keepdims=True)


def reciprocal(values):
    return pl.reciprocal(values, approx=True)


def fetched(source, target, sem):
    copy = pltpu.make_async_copy(source, target, sem)
    copy.start()
    return copy


def as_row(column):
    return jnp.transpose(jnp.broadcast_to(column, (column.shape[0], 128)))[0:1, :]


def iota(shape, dim):
    return lax.broadcasted_iota(jnp.int32, shape, dim)


def extras_kernel(chunk, matches_ref, out_ref):
    high_count = out_ref.shape[0]

    def step(i, total):
        for side in range(2):
            ids = matches_ref[side : side + 1, pl.ds(pl.multiple_of(i * chunk, chunk), chunk)]
            high = lax.shift_right_logical(ids, 7)
            low = jnp.bitwise_and(ids, 127)
            high_hot = jnp.where(iota((high_count, chunk), 0) == high, 1.0, 0.0).astype(BF16)
            low_hot = jnp.where(iota((128, chunk), 0) == low, 1.0, 0.0).astype(BF16)
            total = total + dot(high_hot, low_hot, NT)
        return total

    steps = matches_ref.shape[1] // chunk
    counts = lax.fori_loop(0, steps, step, jnp.zeros(out_ref.shape, F32))
    out_ref[...] = 0.1 + 0.5 * counts


def match_extras(matches, candidates):
    total = matches.shape[0]
    return pl.pallas_call(
        functools.partial(extras_kernel, min(total, 1024)),
        out_shape=jax.ShapeDtypeStruct((candidates // 128, 128), F32),
        in_specs=[pl.BlockSpec(memory_space=pltpu.VMEM)],
        out_specs=pl.BlockSpec(memory_space=pltpu.VMEM),
        cost_estimate=pl.CostEstimate(
            flops=8_000_000_000, bytes_accessed=total * 8, transcendentals=0
        ),
        compiler_params=pltpu.CompilerParams(vmem_limit_bytes=VMEM_BYTES),
        name="match_extras",
    )(matches.T)


def factor_block(diagonal, store):
    count = BLOCK // GROUP
    shape = (GROUP, BLOCK)
    sub = iota(shape, 0)
    lane = iota(shape, 1)
    rows = [diagonal[GROUP * i : GROUP * (i + 1), :] for i in range(count)]

    def column(values, index):
        return jnp.broadcast_to(values[:, index : index + 1], shape)

    def line(values, index):
        return jnp.broadcast_to(values[index : index + 1, :], shape)

    def pick(flags, values):
        result = values[0]
        for flag, value in zip(flags[1:], values[1:]):
            result = jnp.where(flag, value, result)
        return result

    at = [sub == j for j in range(GROUP)]
    for m in range(count):
        start = GROUP * m
        inside = (lane >= start) & (lane < start + GROUP)
        cols = [column(rows[m], start + b) for b in range(GROUP)]
        cell = {(a, b): line(cols[b], a) for b in range(GROUP) for a in range(b + 1)}
        held = jnp.where(inside, jnp.where(lane == start + sub, 1.0, 0.0), rows[m])
        lines = [line(held, j) for j in range(GROUP)]
        band_end = (m * GROUP // BAND + 1) * BAND
        last = (m + 1) * GROUP == band_end
        if start % BAND == 0:
            band = []
        if not last:
            near = [column(rows[m + 1], start + b) for b in range(GROUP)]
            change = None
        scaled_lines, factors, solved_lines, pivots = [], {}, [], []
        for j in range(0, GROUP, 2):
            top, cross, low = cell[j, j], cell[j, j + 1], cell[j + 1, j + 1]
            det = top * low - cross * cross
            inverse = reciprocal(det)
            tops, crosses, lows = top * inverse, cross * inverse, low * inverse
            for b in range(j + 2, GROUP):
                u, v = cell[j, b], cell[j + 1, b]
                factors[j, b] = u * lows - v * crosses
                factors[j + 1, b] = v * tops - u * crosses
            for b in range(j + 2, GROUP):
                for a in range(j + 2, b + 1):
                    part = factors[j, a] * cell[j, b] + factors[j + 1, a] * cell[j + 1, b]
                    cell[a, b] = cell[a, b] - part
            if not last:
                weight1 = near[j] * lows - near[j + 1] * crosses
                weight2 = near[j + 1] * tops - near[j] * crosses
                part = weight1 * lines[j] + weight2 * lines[j + 1]
                change = part if change is None else change + part
                for b in range(j + 2, GROUP):
                    near[b] = near[b] - (near[j] * factors[j, b] + near[j + 1] * factors[j + 1, b])
            for b in range(j + 2, GROUP):
                part = factors[j, b] * lines[j] + factors[j + 1, b] * lines[j + 1]
                lines[b] = lines[b] - part
            solved_lines.append(lines[j] * lows - lines[j + 1] * crosses)
            solved_lines.append(lines[j + 1] * tops - lines[j] * crosses)
            top_inverse = reciprocal(top)
            scaled_lines += [lines[j], lines[j + 1] - cross * top_inverse * lines[j]]
            pivots += [top, det * top_inverse]
        done = pick(at, scaled_lines) * lax.rsqrt(pick(at, pivots))
        store(m, jnp.where(lane < start + GROUP, done, 0.0))
        band.append(jnp.where((lane >= start + GROUP) & (lane < band_end), 0.0, done))
        if not last:
            rows[m + 1] = jnp.where(inside, 0.0, rows[m + 1]) - change
            others = range(m + 2, band_end // GROUP)
            for j in range(GROUP - 4, -1, -2) if len(others) > 0 else ():
                for b in range(j + 2, GROUP):
                    solved_lines[j] = solved_lines[j] - factors[j, b] * solved_lines[b]
                    solved_lines[j + 1] = solved_lines[j + 1] - factors[j + 1, b] * solved_lines[b]
            for i in others:
                terms = [column(rows[i], start + j) * solved_lines[j] for j in range(GROUP)]
                while len(terms) > 1:
                    terms = [a + b for a, b in zip(terms[0::2], terms[1::2])]
                rows[i] = jnp.where(inside, 0.0, rows[i]) - terms[0]
        elif m + 1 < count:
            finished = split(jnp.concatenate(band, axis=0))
            held_out = (lane >= band_end - BAND) & (lane < band_end)
            rest = [jnp.where(held_out, rows[i], 0.0) for i in range(m + 1, count)]
            factor = dot3(split(jnp.concatenate(rest, axis=0)), finished, NT)
            change = dot3(split(factor), finished, NN)
            for i in range(m + 1, count):
                first = GROUP * (i - m - 1)
                rows[i] = jnp.where(held_out, 0.0, rows[i]) - change[first : first + GROUP, :]


def lower_kernel(cols, layers, share, place_ref, *refs):
    pieces = refs[: cols * LAYER]
    extra_ref, high_ref, low_ref, sq_ref, panel_ref = refs[cols * LAYER : cols * LAYER + 5]
    panel, work, ahead, inv, inv_high, inv_low, sq_col, sems, panel_sem = refs[cols * LAYER + 5 :]
    size = work.shape[0]
    row = place_ref[0]
    layer, spot = lax.div(row, LAYER), lax.rem(row, LAYER)
    copies = []
    for e in range(cols):
        for d in range(LAYER):
            for back in range(layers):
                from_spot = spot + d - 2 * jnp.bitwise_and(spot, d)
                block = lax.rem(layer - back + layers, layers) * LAYER + from_spot
                there = pl.ds(pl.multiple_of(block * share, share), share)
                copies.append(
                    fetched(
                        pieces[e * LAYER + d].at[back * share : (back + 1) * share, :],
                        panel.at[e, there, :],
                        sems.at[len(copies)],
                    )
                )
    for copy in copies:
        copy.wait()
    saved = fetched(panel, panel_ref, panel_sem)
    tile = CHUNK
    for r in range(size // tile):
        rows = slice(r * tile, (r + 1) * tile)
        total = half_squares(panel[0, rows, :])
        for e in range(1, cols):
            total = total + half_squares(panel[e, rows, :])
        sq_col[rows, :] = jnp.broadcast_to(total, (tile, 128))
    sq_ref[...] = jnp.transpose(sq_col[...])[0:8, :]
    for r in range(size // tile):
        rows = slice(r * tile, (r + 1) * tile)
        inner = dot(panel[0, rows, :], panel[0], NT)
        for e in range(1, cols):
            inner = inner + dot(panel[e, rows, :], panel[e], NT)
        block = jnp.exp(inner - sq_col[rows, 0:1] - sq_ref[0:1, :])
        on_diagonal = iota((tile, size), 0) + r * tile == iota((tile, size), 1)
        work[rows, :] = block + jnp.where(on_diagonal, extra_ref[...], 0.0)

    steps = size // BLOCK

    def place_of(k):
        return pl.ds(pl.multiple_of(k * BLOCK, BLOCK), BLOCK)

    def store(m, values):
        inv[GROUP * m : GROUP * (m + 1), :] = values

    def look_ahead(k):
        here, there = place_of(k), place_of(lax.rem(k + 1, steps))
        inverse = split(inv[...])
        inv_high[...], inv_low[...] = inverse
        factor = split(dot3(split(work[there, here]), inverse, NT))
        ahead[...] = work[there, there] - dot3(factor, factor, NT)

    def finish_line(k):
        here = place_of(k)
        inverse = (inv_high[...], inv_low[...])
        line = dot3(inverse, split(work[here, :]), NN)
        inside = lax.shift_right_logical(iota((BLOCK, size), 1), 7) == k
        whole = inv_high[...].astype(F32) + inv_low[...].astype(F32)
        line = jnp.where(inside, jnp.concatenate([whole] * steps, axis=1), line)
        work[here, :] = line
        return split(line)

    factor_block(work[0:BLOCK, 0:BLOCK], store)
    look_ahead(0)

    def eliminate(k, carry):
        here = place_of(k - 1)
        diagonal = ahead[...]
        inverse = (inv_high[...], inv_low[...])
        line = finish_line(k - 1)
        inside = lax.shift_right_logical(iota((1, size), 1), 7) == k - 1
        for d in range(steps - 1):
            there = place_of(lax.rem(k + d, steps))
            valid = k + d < steps
            factor = dot3(split(work[there, here]), inverse, NT)
            factor = split(jnp.where(valid, factor, 0.0))
            keep = jnp.where(inside & valid, 0.0, 1.0)
            work[there, :] = work[there, :] * keep - dot3(factor, line, NN)
        factor_block(diagonal, store)
        look_ahead(k)
        return carry

    lax.fori_loop(1, steps, eliminate, 0)
    finish_line(steps - 1)
    for r in range(steps):
        rows = slice(r * BLOCK, (r + 1) * BLOCK)
        kept = iota((BLOCK, size), 0) + r * BLOCK >= iota((BLOCK, size), 1)
        high_ref[rows, :], low_ref[rows, :] = split(jnp.where(kept, work[rows, :], 0.0))
    saved.wait()


def inverse_lower(place, pieces, panel_extra, share):
    size = panel_extra.shape[1]
    cols = len(pieces)
    held, width = pieces[0][0].shape
    layers = held // share
    flat = [piece for group in pieces for piece in group]
    vmem = pl.BlockSpec(memory_space=pltpu.VMEM)
    anywhere = pl.BlockSpec(memory_space=pl.ANY)
    return pl.pallas_call(
        functools.partial(lower_kernel, cols, layers, share),
        out_shape=(
            jax.ShapeDtypeStruct((size, size), BF16),
            jax.ShapeDtypeStruct((size, size), BF16),
            jax.ShapeDtypeStruct((8, size), F32),
            jax.ShapeDtypeStruct((cols, size, width), BF16),
        ),
        in_specs=[pl.BlockSpec(memory_space=pltpu.SMEM)] + [anywhere] * len(flat) + [vmem],
        out_specs=(vmem, vmem, vmem, anywhere),
        scratch_shapes=[
            pltpu.VMEM((cols, size, width), BF16),
            pltpu.VMEM((size, size), F32),
            pltpu.VMEM((BLOCK, BLOCK), F32),
            pltpu.VMEM((BLOCK, BLOCK), F32),
            pltpu.VMEM((BLOCK, BLOCK), BF16),
            pltpu.VMEM((BLOCK, BLOCK), BF16),
            pltpu.VMEM((size, 128), F32),
            pltpu.SemaphoreType.DMA((cols * LAYER * layers,)),
            pltpu.SemaphoreType.DMA,
        ],
        cost_estimate=pl.CostEstimate(
            flops=50_000_000_000, bytes_accessed=8 * size * size, transcendentals=size * size
        ),
        compiler_params=pltpu.CompilerParams(vmem_limit_bytes=VMEM_BYTES),
        name="inverse_lower",
    )(place, *flat, panel_extra)


def solved(values, high_ref, low_ref):
    high, low = split(values)
    size = high.shape[1]
    parts = []
    for j in range(size // CHUNK):
        upto = CHUNK * (j + 1)
        rows = slice(CHUNK * j, upto)
        inverse = (high_ref[rows, :upto], low_ref[rows, :upto])
        parts.append(dot3((high[:, :upto], low[:, :upto]), inverse, NT))
    return jnp.concatenate(parts, axis=1)


def panel_rows(x_ref, rows, panel, features, half, sq_row):
    inner = None
    width = panel.shape[2]
    for e, start in enumerate(features):
        lanes = pl.ds(pl.multiple_of(start * width, width), width)
        part = dot(x_ref[rows, lanes], panel[e], NT)
        inner = part if inner is None else inner + part
    return jnp.exp(inner - half - sq_row)


def panel_hits(values, first_local, row, share, extra_ref):
    local = iota(values.shape, 0) + first_local
    hit = (local + row * share == iota(values.shape, 1)) & (local < share)
    return values + jnp.where(hit, extra_ref[...], 0.0)


def own_kernel(cols, share, place_ref, *refs):
    slices = refs[:cols]
    panel_hbm, high_hbm, low_hbm, sq_ref, panel_extra_ref, own_extra_ref = refs[cols : cols + 6]
    out_hbm, factor_hbm, block_high_hbm, block_low_hbm, half_ref = refs[cols + 6 : cols + 11]
    held, panel, high, low, block_high, block_low, factor, tiles, sems = refs[cols + 11 :]
    row, col = place_ref[0], place_ref[1]
    count = held.shape[0] // cols
    chunk = min(CHUNK, count)
    places = [lax.rem(col - d + cols, cols) for d in range(cols)]
    starts = [pl.multiple_of(place * count, count) for place in places]

    copies = [fetched(slices[0], held.at[0:count, :], sems.at[0])]
    copies.append(fetched(panel_hbm, panel, sems.at[1]))
    copies += [fetched(high_hbm, high, sems.at[2]), fetched(low_hbm, low, sems.at[3])]
    for d in range(1, cols):
        copies.append(fetched(slices[d], held.at[d * count : (d + 1) * count, :], sems.at[3 + d]))
    per = count // chunk
    block_rows = cols * count
    for copy in copies[:2] + copies[4:]:
        copy.wait()
    sq_row = sq_ref[0:1, :]

    def first_row(r):
        place = lax.rem(col - lax.div(r, per) + cols, cols)
        return pl.multiple_of(place * count + lax.rem(r, per) * chunk, chunk)

    def rows_step(r, carry):
        rows = pl.ds(pl.multiple_of(r * chunk, chunk), chunk)
        first = first_row(r)
        there = pl.ds(first, chunk)
        half = half_squares(held[rows, :])
        half_ref[there, :] = jnp.broadcast_to(half, (chunk, 128))
        block = panel_rows(held, rows, panel, places, half, sq_row)
        block = panel_hits(block, first, row, share, panel_extra_ref)

        @pl.when(r == 0)
        def _():
            copies[2].wait()
            copies[3].wait()

        values = solved(block, high, low)
        factor[rows, :] = values
        block_high[there, :], block_low[there, :] = split(values)
        return carry

    lax.fori_loop(0, cols * per, rows_step, 0)
    outs = [
        fetched(factor.at[0:count, :], factor_hbm, sems.at[4 + cols]),
        fetched(block_high, block_high_hbm, sems.at[5 + cols]),
        fetched(block_low, block_low_hbm, sems.at[6 + cols]),
    ]
    mine = pl.ds(starts[0], count)
    own_row = as_row(half_ref[mine, 0:1])

    def tile_step(r, carry):
        rows = pl.ds(pl.multiple_of(r * chunk, chunk), chunk)
        there = pl.ds(first_row(r), chunk)
        inner = dot(held[rows, :], held[0:count, :], NT)
        values = jnp.exp(inner - half_ref[there, 0:1] - own_row)
        own_factor = (block_high[mine, :], block_low[mine, :])
        values = values - dot3((block_high[there, :], block_low[there, :]), own_factor, NT)
        same = iota((chunk, count), 0) + r * chunk == iota((chunk, count), 1)
        tiles[there, :] = values + jnp.where(same, own_extra_ref[...], 0.0)
        return carry

    lax.fori_loop(0, cols * per, tile_step, 0)
    outs.append(fetched(tiles, out_hbm.at[:, 0:count], sems.at[3 + cols]))
    for copy in outs:
        copy.wait()


def own_rows(place, slices, panel, high, low, sq, panel_extra, own_extra, share):
    cols = len(slices)
    (count, embed), size = slices[0].shape, high.shape[0]
    block_rows = count * cols
    vmem = pl.BlockSpec(memory_space=pltpu.VMEM)
    anywhere = pl.BlockSpec(memory_space=pl.ANY)
    return pl.pallas_call(
        functools.partial(own_kernel, cols, share),
        out_shape=(
            jax.ShapeDtypeStruct((block_rows, STOPS * count), F32),
            jax.ShapeDtypeStruct((count, size), F32),
            jax.ShapeDtypeStruct((block_rows, size), BF16),
            jax.ShapeDtypeStruct((block_rows, size), BF16),
            jax.ShapeDtypeStruct((block_rows, 128), F32),
        ),
        in_specs=[pl.BlockSpec(memory_space=pltpu.SMEM)] + [anywhere] * (cols + 3) + [vmem] * 3,
        out_specs=(anywhere, anywhere, anywhere, anywhere, vmem),
        scratch_shapes=[
            pltpu.VMEM((block_rows, embed), BF16),
            pltpu.VMEM(panel.shape, BF16),
            pltpu.VMEM((size, size), BF16),
            pltpu.VMEM((size, size), BF16),
            pltpu.VMEM((block_rows, size), BF16),
            pltpu.VMEM((block_rows, size), BF16),
            pltpu.VMEM((block_rows, size), F32),
            pltpu.VMEM((block_rows, count), F32),
            pltpu.SemaphoreType.DMA((cols + 7,)),
        ],
        cost_estimate=pl.CostEstimate(
            flops=block_rows * size, bytes_accessed=block_rows * size, transcendentals=0
        ),
        compiler_params=pltpu.CompilerParams(vmem_limit_bytes=VMEM_BYTES),
        name="own_rows",
    )(place, *slices, panel, high, low, sq, panel_extra, own_extra)


def visit_kernel(cols, share, routes, place_ref, *refs):
    sources = sorted({name for route in routes for pick in route for name, _ in pick[1]})
    arrivals = dict(zip(sources, refs[: len(sources)]))
    slices = refs[len(sources) : len(sources) + cols]
    rest = refs[len(sources) + cols :]
    panel_hbm, high_hbm, low_hbm, block_high_hbm, block_low_hbm = rest[:5]
    sq_ref, half_ref, panel_extra_ref = rest[5:8]
    out_hbm = rest[9]
    seen, held, panel, high, low, block_high, block_low = rest[10:17]
    seen_high, seen_low, visit_half, tiles, sems = rest[17:]
    size = high.shape[0]
    row_count = size // share
    row, col = place_ref[0], place_ref[1]
    spot = lax.rem(row, LAYER)
    count = seen.shape[1]
    chunk = min(CHUNK, count)
    places = [lax.rem(col - d + cols, cols) for d in range(cols)]
    visits = len(routes)

    def arrive(v):
        for spots, parts, _ in routes[v]:
            chosen = spot == spots[0]
            for other in spots[1:]:
                chosen = chosen | (spot == other)

            @pl.when(chosen)
            def _():
                first = 0
                for name, length in parts:
                    pltpu.make_async_copy(
                        arrivals[name].at[0:length, :],
                        seen.at[v, first : first + length, :],
                        sems.at[v],
                    ).start()
                    first += length

    def arrived(v):
        pltpu.make_async_copy(seen.at[v], seen.at[v], sems.at[v]).wait()

    arrive(0)
    loads = [fetched(panel_hbm, panel, sems.at[visits])]
    loads.append(fetched(high_hbm, high, sems.at[visits + 1]))
    loads.append(fetched(low_hbm, low, sems.at[visits + 2]))
    for d in range(cols):
        piece = held.at[d * count : (d + 1) * count, :]
        loads.append(fetched(slices[d], piece, sems.at[visits + 3 + d]))
    loads.append(fetched(block_high_hbm, block_high, sems.at[visits + 3 + cols]))
    loads.append(fetched(block_low_hbm, block_low, sems.at[visits + 4 + cols]))
    for v in range(1, visits):
        arrive(v)
    sq_row = sq_ref[0:1, :]
    per = count // chunk

    def first_row(r):
        place = lax.rem(col - lax.div(r, per) + cols, cols)
        return pl.multiple_of(place * count + lax.rem(r, per) * chunk, chunk)

    def stop_of(v):
        stop = jnp.int32(0)
        for i, route in enumerate(routes):
            for spots, _, at_stop in route:
                for one in spots:
                    stop = jnp.where((spot == one) & (v == i), at_stop, stop)
        return stop

    def out_copy(v):
        first = pl.multiple_of(stop_of(v) * count, count)
        target = out_hbm.at[:, pl.ds(first, count)]
        return pltpu.make_async_copy(tiles.at[v], target, sems.at[visits + 5 + cols + v])

    loads[0].wait()

    def visit_step(v, carry):
        visit_row = lax.rem(row - stop_of(v) + row_count, row_count)
        arrived(v)
        visit_half[...] = jnp.broadcast_to(half_squares(seen[v]), (count, 128))

        def rows_step(r, carry):
            rows = pl.ds(pl.multiple_of(r * chunk, chunk), chunk)
            block = panel_rows(seen.at[v], rows, panel, places, visit_half[rows, 0:1], sq_row)
            block = panel_hits(block, col * count + r * chunk, visit_row, share, panel_extra_ref)

            @pl.when((v == 0) & (r == 0))
            def _():
                loads[1].wait()
                loads[2].wait()

            seen_high[rows, :], seen_low[rows, :] = split(solved(block, high, low))
            return carry

        lax.fori_loop(0, per, rows_step, 0)

        @pl.when(v == 0)
        def _():
            for load in loads[3:]:
                load.wait()

        visit_line = as_row(visit_half[:, 0:1])

        def tile_step(r, carry):
            rows = pl.ds(pl.multiple_of(r * chunk, chunk), chunk)
            there = pl.ds(first_row(r), chunk)
            inner = dot(held[rows, :], seen[v], NT)
            values = jnp.exp(inner - half_ref[there, 0:1] - visit_line)
            factor = (seen_high[...], seen_low[...])
            part = dot3((block_high[there, :], block_low[there, :]), factor, NT)
            tiles[v, there, :] = values - part
            return carry

        lax.fori_loop(0, cols * per, tile_step, 0)
        out_copy(v).start()
        return carry

    lax.fori_loop(0, visits, visit_step, 0)
    for v in range(visits):
        out_copy(v).wait()


def visit(name, routes, share, place, arrivals, slices, panel, own, panel_extra, trailing):
    sources = sorted({source for route in routes for pick in route for source, _ in pick[1]})
    cols = len(slices)
    (count, embed), visits = slices[0].shape, len(routes)
    block_rows = count * cols
    high, low, sq, block_high, block_low, half = own
    size = high.shape[0]
    vmem = pl.BlockSpec(memory_space=pltpu.VMEM)
    anywhere = pl.BlockSpec(memory_space=pl.ANY)
    moved = len(sources) + cols + 5
    return pl.pallas_call(
        functools.partial(visit_kernel, cols, share, routes),
        out_shape=jax.ShapeDtypeStruct(trailing.shape, F32),
        in_specs=[pl.BlockSpec(memory_space=pltpu.SMEM)]
        + [anywhere] * moved
        + [vmem] * 3
        + [anywhere],
        out_specs=anywhere,
        scratch_shapes=[
            pltpu.VMEM((visits, count, embed), BF16),
            pltpu.VMEM((block_rows, embed), BF16),
            pltpu.VMEM(panel.shape, BF16),
            pltpu.VMEM((size, size), BF16),
            pltpu.VMEM((size, size), BF16),
            pltpu.VMEM((block_rows, size), BF16),
            pltpu.VMEM((block_rows, size), BF16),
            pltpu.VMEM((count, size), BF16),
            pltpu.VMEM((count, size), BF16),
            pltpu.VMEM((count, 128), F32),
            pltpu.VMEM((visits, block_rows, count), F32),
            pltpu.SemaphoreType.DMA((2 * visits + 5 + cols,)),
        ],
        input_output_aliases={1 + moved + 3: 0},
        cost_estimate=pl.CostEstimate(
            flops=count * size, bytes_accessed=count * size, transcendentals=0
        ),
        compiler_params=pltpu.CompilerParams(vmem_limit_bytes=VMEM_BYTES),
        name=name,
    )(
        place,
        *[arrivals[source] for source in sources],
        *slices,
        panel,
        high,
        low,
        block_high,
        block_low,
        sq,
        half,
        panel_extra,
        trailing,
    )


def sent(block, pairs):
    return lax.ppermute(block, "row", pairs)


def after(value, *others):
    return lax.optimization_barrier((value,) + others)[0]


def body(embeddings, inverse_scales, matches):
    row_count = lax.axis_size("row")
    col_count = lax.axis_size("col")
    row_index = lax.axis_index("row")
    col_index = lax.axis_index("col")
    slice_rows, embed = embeddings.shape
    block_rows = slice_rows * col_count
    share = PANEL // row_count
    width = embed // col_count
    layers = row_count // LAYER
    rows = range(row_count)
    place = jnp.stack([row_index, col_index]).astype(jnp.int32)

    def spots(*wanted):
        return [r for r in rows if r % LAYER in wanted]

    def up(r):
        return (r + LAYER) % row_count

    part = jnp.where(col_index == 0, embeddings[:share, :width], jnp.zeros((share, width), BF16))
    for c in range(1, col_count):
        given = lax.ppermute(embeddings[:share, c * width : (c + 1) * width], "col", [(0, c)])
        part = jnp.where(col_index == c, given, part)
    own_scales = lax.dynamic_slice(inverse_scales, (col_index * width,), (width,))
    part = (part.astype(F32) * own_scales[None, :]).astype(BF16)
    scaled = (embeddings.astype(F32) * inverse_scales[None, :]).astype(BF16)
    column = [part]
    for back in range(1, layers):
        column.append(sent(part, [(r, (r + back * LAYER) % row_count) for r in rows]))
    column = jnp.concatenate(column, axis=0)
    extras = match_extras(after(matches, column), row_count * block_rows)
    gathered = [column] + [sent(column, [(r, r ^ d) for r in rows]) for d in range(1, LAYER)]
    gathered[1:] = [after(piece, extras, scaled) for piece in gathered[1:]]
    pieces = [gathered]
    for c in range(1, col_count):
        pieces.append([rotated(piece, "col", c) for piece in gathered])
    slices = [scaled] + [rotated(scaled, "col", d) for d in range(1, col_count)]

    extras = extras.reshape(row_count, block_rows)
    panel_extra = extras[:, :share].reshape(1, PANEL)
    own_extra = lax.dynamic_slice(
        extras, (row_index, col_index * slice_rows), (1, slice_rows)
    )

    rising = after(scaled, column)
    above = sent(rising, [(r, up(r)) for r in spots(1, 2, 3)])
    leaving = after(scaled, *gathered[1:])
    beside = sent(leaving, [(r, r ^ 1) for r in rows])
    across = sent(leaving, [(r, r ^ 2) for r in rows])

    high, low, sq, panel = inverse_lower(place, pieces, panel_extra, share)

    mid = slice_rows // 2
    spot = lax.rem(row_index, LAYER)
    beside2, across2, above2 = (after(block, high) for block in (beside, across, above))
    up2 = jnp.where(spot == 1, across2[:mid], beside2[mid:])
    x2 = jnp.where(spot == 2, across2[mid:], above2[:mid])
    y2 = jnp.where(spot == 2, above2[:mid], jnp.where(spot == 3, above2[mid:], beside2[:mid]))
    up2 = sent(up2, [(r, up(r)) for r in rows])
    x2 = sent(x2, [(r, r ^ 1) for r in spots(1, 2, 3)])
    y2 = sent(y2, [(r, r ^ 2) for r in rows])

    trailing, factor, block_high, block_low, half = own_rows(
        place, slices, panel, high, low, sq, panel_extra, own_extra, share
    )
    up2, x2, y2, half = lax.optimization_barrier((up2, x2, y2, half))
    x3 = jnp.where(spot == 1, up2, jnp.where(spot == 0, y2, across2[mid:]))
    up3 = sent(across2[mid:], [(r, up(r)) for r in spots(0)])
    x3 = sent(x3, [(r, r ^ 1) for r in spots(0, 1, 3)])
    y3 = sent(up2, [(r, r ^ 2) for r in spots(2, 3)])
    arrivals = {
        "across": across,
        "beside": beside,
        "up2": up2,
        "x2": x2,
        "y2": y2,
        "up3": up3,
        "x3": x3,
        "y3": y3,
    }

    def halves(low_half, high_half):
        return ((low_half, mid), (high_half, slice_rows - mid))

    def whole(block):
        return ((block, slice_rows),)

    first = (
        ((0,), halves("x2", "up2"), 3),
        ((1, 3), whole("beside"), 1),
        ((2,), whole("across"), 2),
    )
    second = (
        ((0,), halves("y2", "up3"), 2),
        ((1,), halves("up2", "y2"), 2),
        ((2,), halves("x2", "up2"), 3),
        ((3,), whole("across"), 2),
    )
    third = (
        ((0,), halves("x3", "y3"), 1),
        ((1,), halves("x3", "y3"), 3),
        ((2,), halves("y2", "x3"), 1),
        ((3,), halves("y2", "x2"), 3),
    )
    own = (high, low, sq, block_high, block_low, half)
    rest = (slices, panel, own, panel_extra)
    trailing = visit("visit_first", (first,), share, place, arrivals, *rest, trailing)
    trailing = visit("visit_rest", (second, third), share, place, arrivals, *rest, trailing)
    return (trailing, factor)


def solution(mesh):
    return jax.shard_map(
        body,
        mesh=mesh,
        in_specs=(P(("row", "col"), None), P(), P()),
        out_specs=(P("row", "col"), P(("row", "col"), None)),
        check_vma=False,
    )
```

time: 807 us -> 234 us (0.29)
  other arithmetic: 294 us -> 9.99 us
  waiting for transfers between devices: 297 us -> 32.1 us
  Pallas kernels: 0 us -> 155 us
  matrix products: 110 us -> 0 us
  local copies, waits for them, and re-layouts: 71.5 us -> 4.78 us
  starting transfers between devices: 5.8 us -> 29.9 us
  between operations: 19.4 us -> 1.07 us
    another operation x33 -> x1, other arithmetic: 256 us -> 0.58 us  [body(): place = jnp.stack([row_index, col_index]).astype(jnp.int32)]
    all_gather x4 -> x0, waiting for transfers between devices: 158 us -> none  [the longest x1 74.6 us: body(): panel_scaled = lax.all_gather(lead_scaled, 'row', axis=0, tiled=True)]
    pallas_call x0 -> x5, Pallas kernels: none -> 155 us  [the longest x1 72.7 us: inverse_lower(): pl.pallas_call(functools.partial(lower_kernel, cols, layers, share), out_...]
    ppermute x6 -> x21, waiting for transfers between devices: 139 us -> 32.1 us  [the longest x15 31.8 us: sent(): return lax.ppermute(block, 'row', pairs)]
    dot_general x10 -> x0, matrix products: 62.8 us -> none  [the longest x4 36.2 us: stop_tile(): jnp.dot(block_factor, visit_factor.T, precision=lax.Precision.HIGHEST)]
    another operation x29 -> x0, matrix products: 47.5 us -> none  [the longest x15 24.5 us: solve_rows(): lax.linalg.triangular_solve(lower, rows, left_side=False, lower=True, tra...]
    reduce_sum x38 -> x0, other arithmetic: 28.6 us -> none  [the longest x6 14.6 us: squares_of(): return jnp.sum(values * values, axis=1)]
    another operation x33 -> x0, local copies, waits for them, and re-layouts: 25.3 us -> none
  transfers between devices with their start and end apart: 10 -> 21, of which waited for: 7 -> 7; matrix products, arithmetic and copies ran while one was open for 56% -> 5% of each run, Pallas kernels for 0% -> 53%
where the time goes in v1:
time: 234 us; the launch traced here: 233 us
  Pallas kernels  155 us (66%)
  waiting for transfers between devices  32.1 us (14%)
  starting transfers between devices  29.9 us (13%)
  other arithmetic  9.99 us (4%)
  local copies, waits for them, and re-layouts  4.78 us (2%)
    pallas_call x1, Pallas kernels, inverse_lower(): pl.pallas_call(functools.partial(lower_kernel, cols, layers, share), out_...  72.7 us
    pallas_call x2, Pallas kernels, visit(): pl.pallas_call(functools.partial(visit_kernel, cols, share, routes), out_...  49.3 us
    ppermute x15, waiting for transfers between devices, sent(): return lax.ppermute(block, 'row', pairs)  31.8 us
    pallas_call x1, Pallas kernels, own_rows(): pl.pallas_call(functools.partial(own_kernel, cols, share), out_shape=(jax...  26.7 us
    ppermute x15, starting transfers between devices, sent(): return lax.ppermute(block, 'row', pairs)  26.4 us
    pallas_call x1, Pallas kernels, match_extras(): pl.pallas_call(functools.partial(extras_kernel, min(total, 1024)), out_sh...  6.66 us
    select_n x1, other arithmetic, body(): jnp.where(spot == 2, above2[:mid], jnp.where(spot == 3, above2[mid:], bes...  4.87 us
  transfers between devices with their start and end apart: 21, of which 7 were waited for; matrix products, arithmetic and copies ran while one was open for 5% of the time, Pallas kernels for 53%

profile of v1, /device:TPU:0, one launch (start us, length us, event | category | flops | bytes accessed | tf_op | source)
XLA Modules:
  0.0 233.1 jit_solution(5821496856820025988)
XLA Ops:
  0.6 0.9 slice.30
  1.5 2.4 %collective-permute-start = (bf16[64,1024]{1,0:T(8,128)(2,1)S(1)}, bf16[64,1024]{1,0:T(8,128)(2,1)S(1)}, u32[]{:S(2)}, u32[]{:S(2)}) collective-permute-start(bf16[64,1024]{1,0:T(8,128)(2,1)S(1)} %slice.30), channel_id=1, source_target_pairs={{0,1},{2,3},{4,5},{6,7},{8,9},{10,11},{12,13},{14,15},{16,17},{18,... | collective-permute-start | bytes 393224 | tf_op jit(solution)/shard_map/ppermute | solution.py:658
  3.9 0.7 dynamic_slice.6
  4.6 0.3 collective-permute-done
  4.9 1.0 multiply_convert_fusion.1
  5.8 4.5 %collective-permute-start.3 = (bf16[64,1024]{1,0:T(8,128)(2,1)S(1)}, bf16[64,1024]{1,0:T(8,128)(2,1)S(1)}, u32[]{:S(2)}, u32[]{:S(2)}) collective-permute-start(bf16[64,1024]{1,0:T(8,128)(2,1)S(1)} %multiply_convert_fusion.1), channel_id=1, source_target_pairs={{0,24},{2,26},{4,28},{6,30},{8,0},{10,2},{12,4},{14,6},{16,8},{18,... | collective-permute-start | bytes 393224 | tf_op jit(solution)/shard_map/ppermute | solution.py:630
  10.3 0.0 collective-permute-start.2
  10.3 1.0 collective-permute-start.1
  11.4 2.1 multiply_convert_fusion.refs_0_.refs_4_.refs_7_
  13.5 0.7 collective-permute-done.3
  14.3 8.1 %collective-permute-done.2 = bf16[64,1024]{1,0:T(8,128)(2,1)S(1)} collective-permute-done((bf16[64,1024]{1,0:T(8,128)(2,1)S(1)}, bf16[64,1024]{1,0:T(8,128)(2,1)S(1)}, u32[]{:S(2)}, u32[]{:S(2)}) %collective-permute-start.2) | collective-permute-done | bytes 131104 | tf_op jit(solution)/shard_map/ppermute | solution.py:630
  22.4 0.0 copy-start.8
  22.4 0.1 collective-permute-start.8
  22.5 2.5 %collective-permute-start.6 = (bf16[256,1024]{1,0:T(8,128)(2,1)S(1)}, bf16[256,1024]{1,0:T(8,128)(2,1)}, u32[]{:S(2)}, u32[]{:S(2)}) collective-permute-start(bf16[256,1024]{1,0:T(8,128)(2,1)S(1)} %pad_maximum_fusion.refs_0_), channel_id=1, source_target_pairs={{0,6},{2,4},{4,2},{6,0},{8,14},{10,12},{12,10},{14,8},{16,22},{18,... | collective-permute-start | bytes 1572872 | tf_op jit(solution)/shard_map/ppermute | solution.py:630
  25.0 0.5 collective-permute-start.5
  25.5 0.5 collective-permute-start.4
  26.0 6.7 %match_extras.1 = f32[128,128]{1,0:T(8,128)} custom-call(s32[2,16384]{1,0:T(2,128)} %bitcast.3), custom_call_target="tpu_custom_call" | custom-call | flops 8000000000 | bytes 131072 | tf_op jit(solution)/shard_map/match_extras/pallas_call | solution.py:88
  32.7 5.6 %collective-permute-done.6.refs_3_ = bf16[256,1024]{1,0:T(8,128)(2,1)} collective-permute-done((bf16[256,1024]{1,0:T(8,128)(2,1)S(1)}, bf16[256,1024]{1,0:T(8,128)(2,1)}, u32[]{:S(2)}, u32[]{:S(2)}) %collective-permute-start.6) | collective-permute-done | bytes 524320 | tf_op jit(solution)/shard_map/ppermute | solution.py:630
  38.3 10.8 %collective-permute-done.4.refs_1_ = bf16[256,1024]{1,0:T(8,128)(2,1)} collective-permute-done((bf16[256,1024]{1,0:T(8,128)(2,1)S(1)}, bf16[256,1024]{1,0:T(8,128)(2,1)}, u32[]{:S(2)}, u32[]{:S(2)}) %collective-permute-start.4) | collective-permute-done | bytes 524320 | tf_op jit(solution)/shard_map/ppermute | solution.py:630
  49.1 0.0 collective-permute-start.9
  49.1 0.0 collective-permute-done.5.refs_2_
  49.1 0.5 collective-permute-start.10
  49.7 0.0 collective-permute-start.11
  49.7 0.5 collective-permute-start.17
  50.2 0.6 pad_add_fusion.place_ref
  50.7 0.9 reshape.12
  51.6 0.7 reshape.13.refs_8_.refs_6_.refs_13_.refs_16_
  52.3 2.0 collective-permute-start.14
  54.3 0.0 collective-permute-done.9.refs_5_
  54.3 2.0 collective-permute-start.12
  56.2 0.0 collective-permute-done.10.refs_6_
  56.2 0.5 collective-permute-start.7
  56.8 72.7 %inverse_lower.1 = (bf16[1024,1024]{1,0:T(8,128)(2,1)}, bf16[1024,1024]{1,0:T(8,128)(2,1)}, f32[8,1024]{1,0:T(8,128)}, bf16[2,1024,1024]{2,1,0:T(8,128)(2,1)}) custom-call(s32[2]{0:T(128)} %pad_add_fusion.place_ref, bf16[256,1024]{1,0:T(8,128)(2,1)} %copy-done.8, bf16[256,1024]{1,0:T(8,128)(2,1)} %collective-permute-done.4.refs_1_, ...), custom_call_target="tpu_custom_call" | custom-call | flops 49999998976 | bytes 8388608 | tf_op jit(solution)/shard_map/inverse_lower/pallas_call | solution.py:293
  129.5 4.9 %select_select_fusion.1 = (bf16[256,2048]{1,0:T(8,128)(2,1)}, bf16[256,2048]{1,0:T(8,128)(2,1)}, bf16[256,2048]{1,0:T(8,128)(2,1)}) fusion(bf16[512,2048]{1,0:T(8,128)(2,1)S(1)} %collective-permute-done.12.refs_1_, bf16[512,2048]{1,0:T(8,128)(2,1)} %collective-permute-done.14, pred[]{:T(512)S(6)} %eq.24, pred[]{:T(512)S(6)} %eq.23, ...), kind=kLoop, calls=%fused_computation.2 | loop fusion | flops 2097152 | bytes 9437187 | tf_op jit(solution)/shard_map/jit(_where)/select_n | solution.py:694
  134.4 1.6 collective-permute-start.16
  136.0 1.3 collective-permute-start.15
  137.2 2.5 %collective-permute-start.13 = (bf16[256,2048]{1,0:T(8,128)(2,1)}, bf16[256,2048]{1,0:T(8,128)(2,1)S(1)}, u32[]{:S(2)}, u32[]{:S(2)}) collective-permute-start(bf16[256,2048]{1,0:T(8,128)(2,1)} %get-tuple-element.50), channel_id=1, source_target_pairs={{0,8},{2,10},{4,12},{6,14},{8,16},{10,18},{12,20},{14,22},{16,24},... | collective-permute-start | bytes 3145736 | tf_op jit(solution)/shard_map/ppermute | solution.py:630
  139.8 0.6 dynamic_slice.7.refs_7_
  140.4 26.7 %own_rows.1 = (f32[1024,2048]{1,0:T(8,128)}, f32[512,1024]{1,0:T(8,128)}, bf16[1024,1024]{1,0:T(8,128)(2,1)}, bf16[1024,1024]{1,0:T(8,128)(2,1)}, f32[1024,128]{1,0:T(8,128)}) custom-call(s32[2]{0:T(128)} %pad_add_fusion.place_ref, bf16[512,2048]{1,0:T(8,128)(2,1)} %copy-done, bf16[512,2048]{1,0:T(8,128)(2,1)} %collective-permute-done.17.refs_1_.refs_5_.refs_8_, ...), custom_call_target="tpu_custom_call" | custom-call | flops 1048576 | bytes 1048576 | tf_op jit(solution)/shard_map/own_rows/pallas_call | solution.py:427
  167.1 1.3 collective-permute-start.20
  168.4 1.4 select_select_fusion
  169.9 4.3 %collective-permute-start.19 = (bf16[256,2048]{1,0:T(8,128)(2,1)S(1)}, bf16[256,2048]{1,0:T(8,128)(2,1)S(1)}, u32[]{:S(2)}, u32[]{:S(2)}) collective-permute-start(bf16[256,2048]{1,0:T(8,128)(2,1)S(1)} %get-tuple-element.46), channel_id=1, source_target_pairs={{0,2},{2,0},{6,4},{8,10},{10,8},{14,12},{16,18},{18,16},{22,20},{2... | collective-permute-start | bytes 3145736 | tf_op jit(solution)/shard_map/ppermute | solution.py:630
  174.2 1.9 collective-permute-start.18
  176.1 18.3 %visit_first.1.refs_17_ = f32[1024,2048]{1,0:T(8,128)} custom-call(s32[2]{0:T(128)} %pad_add_fusion.place_ref, bf16[512,2048]{1,0:T(8,128)(2,1)} %copy-done.1, bf16[512,2048]{1,0:T(8,128)(2,1)} %copy-done.4, bf16[256,2048]{1,0:T(8,128)(2,1)} %copy-done.3, bf16[256,2048]{1,0:T(8,128)(2,1)} %collective-permute-done.15.refs_3_, ...), custom_call_target="tpu_custom_call", output_to_operand_aliasing={{}: (15, {})} | custom-call | flops 524288 | bytes 524288 | tf_op jit(solution)/shard_map/visit_first/pallas_call | solution.py:585
  194.4 1.3 collective-permute-done.19.refs_4_
  195.8 5.2 %collective-permute-done.18.refs_2_ = bf16[256,2048]{1,0:T(8,128)(2,1)S(1)} collective-permute-done((bf16[256,2048]{1,0:T(8,128)(2,1)S(1)}, bf16[256,2048]{1,0:T(8,128)(2,1)S(1)}, u32[]{:S(2)}, u32[]{:S(2)}) %collective-permute-start.18) | collective-permute-done | bytes 1048608 | tf_op jit(solution)/shard_map/ppermute | solution.py:630
  201.0 1.0 copy-done.7
  201.9 31.0 %visit_rest.1 = f32[1024,2048]{1,0:T(8,128)} custom-call(s32[2]{0:T(128)} %pad_add_fusion.place_ref, bf16[512,2048]{1,0:T(8,128)(2,1)} %copy-done.1, bf16[256,2048]{1,0:T(8,128)(2,1)} %copy-done.3, bf16[256,2048]{1,0:T(8,128)(2,1)} %copy-done.7, bf16[256,2048]{1,0:T(8,128)(2,1)} %collective-permute-done.15.refs_3_, ...), custom_call_target="tpu_custom_call", output_to_operand_aliasing={{}: (18, {})} | custom-call | flops 524288 | bytes 524288 | tf_op jit(solution)/shard_map/visit_rest/pallas_call | solution.py:585
  (29 shorter events, 0.1 us)
Async XLA Ops:
  1.5 3.3 %collective-permute-start = (bf16[64,1024]{1,0:T(8,128)(2,1)S(1)}, bf16[64,1024]{1,0:T(8,128)(2,1)S(1)}, u32[]{:S(2)}, u32[]{:S(2)}) collective-permute-start(bf16[64,1024]{1,0:T(8,128)(2,1)S(1)} %slice.30), channel_id=1, source_target_pairs={{0,1},{2,3},{4,5},{6,7},{8,9},{10,11},{12,13},{14,15},{16,17},{18,... | collective-permute-start | bytes 393224 | tf_op jit(solution)/shard_map/ppermute | solution.py:658
  5.8 8.4 %collective-permute-start.3 = (bf16[64,1024]{1,0:T(8,128)(2,1)S(1)}, bf16[64,1024]{1,0:T(8,128)(2,1)S(1)}, u32[]{:S(2)}, u32[]{:S(2)}) collective-permute-start(bf16[64,1024]{1,0:T(8,128)(2,1)S(1)} %multiply_convert_fusion.1), channel_id=1, source_target_pairs={{0,24},{2,26},{4,28},{6,30},{8,0},{10,2},{12,4},{14,6},{16,8},{18,... | collective-permute-start | bytes 393224 | tf_op jit(solution)/shard_map/ppermute | solution.py:630
  10.3 12.0 %collective-permute-start.2 = (bf16[64,1024]{1,0:T(8,128)(2,1)S(1)}, bf16[64,1024]{1,0:T(8,128)(2,1)S(1)}, u32[]{:S(2)}, u32[]{:S(2)}) collective-permute-start(bf16[64,1024]{1,0:T(8,128)(2,1)S(1)} %multiply_convert_fusion.1), channel_id=1, source_target_pairs={{0,16},{2,18},{4,20},{6,22},{8,24},{10,26},{12,28},{14,30},{16,0},... | collective-permute-start | bytes 393224 | tf_op jit(solution)/shard_map/ppermute | solution.py:630
  10.3 12.0 %collective-permute-start.1 = (bf16[64,1024]{1,0:T(8,128)(2,1)S(1)}, bf16[64,1024]{1,0:T(8,128)(2,1)S(1)}, u32[]{:S(2)}, u32[]{:S(2)}) collective-permute-start(bf16[64,1024]{1,0:T(8,128)(2,1)S(1)} %multiply_convert_fusion.1), channel_id=1, source_target_pairs={{0,8},{2,10},{4,12},{6,14},{8,16},{10,18},{12,20},{14,22},{16,24},... | collective-permute-start | bytes 393224 | tf_op jit(solution)/shard_map/ppermute | solution.py:630
  13.5 42.7 %copy-start = (bf16[512,2048]{1,0:T(8,128)(2,1)}, bf16[512,2048]{1,0:T(8,128)(2,1)S(1)}, u32[]{:S(2)}) copy-start(bf16[512,2048]{1,0:T(8,128)(2,1)S(1)} %multiply_convert_fusion.refs_0_.refs_4_.refs_7_) | copy-start | bytes 6291460
  22.4 10.3 %copy-start.8 = (bf16[256,1024]{1,0:T(8,128)(2,1)}, bf16[256,1024]{1,0:T(8,128)(2,1)S(1)}, u32[]{:S(2)}) copy-start(bf16[256,1024]{1,0:T(8,128)(2,1)S(1)} %pad_maximum_fusion.refs_0_) | copy-start | bytes 1572868
  22.4 29.9 %collective-permute-start.8 = (bf16[256,1024]{1,0:T(8,128)(2,1)S(1)}, bf16[256,1024]{1,0:T(8,128)(2,1)}, u32[]{:S(2)}, u32[]{:S(2)}) collective-permute-start(bf16[256,1024]{1,0:T(8,128)(2,1)S(1)} %pad_maximum_fusion.refs_0_), channel_id=1, source_target_pairs={{0,1},{1,0},{2,3},{3,2},{4,5},{5,4},{6,7},{7,6},{8,9},{9,8},{10,11... | collective-permute-start | bytes 1572872 | tf_op jit(solution)/shard_map/ppermute | solution.py:27
  22.5 15.8 %collective-permute-start.6 = (bf16[256,1024]{1,0:T(8,128)(2,1)S(1)}, bf16[256,1024]{1,0:T(8,128)(2,1)}, u32[]{:S(2)}, u32[]{:S(2)}) collective-permute-start(bf16[256,1024]{1,0:T(8,128)(2,1)S(1)} %pad_maximum_fusion.refs_0_), channel_id=1, source_target_pairs={{0,6},{2,4},{4,2},{6,0},{8,14},{10,12},{12,10},{14,8},{16,22},{18,... | collective-permute-start | bytes 1572872 | tf_op jit(solution)/shard_map/ppermute | solution.py:630
  25.0 24.2 %collective-permute-start.5 = (bf16[256,1024]{1,0:T(8,128)(2,1)S(1)}, bf16[256,1024]{1,0:T(8,128)(2,1)}, u32[]{:S(2)}, u32[]{:S(2)}) collective-permute-start(bf16[256,1024]{1,0:T(8,128)(2,1)S(1)} %pad_maximum_fusion.refs_0_), channel_id=1, source_target_pairs={{0,4},{2,6},{4,0},{6,2},{8,12},{10,14},{12,8},{14,10},{16,20},{18,... | collective-permute-start | bytes 1572872 | tf_op jit(solution)/shard_map/ppermute | solution.py:630
  25.5 23.7 %collective-permute-start.4 = (bf16[256,1024]{1,0:T(8,128)(2,1)S(1)}, bf16[256,1024]{1,0:T(8,128)(2,1)}, u32[]{:S(2)}, u32[]{:S(2)}) collective-permute-start(bf16[256,1024]{1,0:T(8,128)(2,1)S(1)} %pad_maximum_fusion.refs_0_), channel_id=1, source_target_pairs={{0,2},{2,0},{4,6},{6,4},{8,10},{10,8},{12,14},{14,12},{16,18},{18,... | collective-permute-start | bytes 1572872 | tf_op jit(solution)/shard_map/ppermute | solution.py:630
  49.1 5.1 %collective-permute-start.9 = (bf16[256,1024]{1,0:T(8,128)(2,1)}, bf16[256,1024]{1,0:T(8,128)(2,1)}, u32[]{:S(2)}, u32[]{:S(2)}) collective-permute-start(bf16[256,1024]{1,0:T(8,128)(2,1)} %collective-permute-done.4.refs_1_), channel_id=1, source_target_pairs={{0,1},{1,0},{2,3},{3,2},{4,5},{5,4},{6,7},{7,6},{8,9},{9,8},{10,11... | collective-permute-start | bytes 1572872 | tf_op jit(solution)/shard_map/ppermute | solution.py:27
  49.1 7.1 %collective-permute-start.10 = (bf16[256,1024]{1,0:T(8,128)(2,1)}, bf16[256,1024]{1,0:T(8,128)(2,1)}, u32[]{:S(2)}, u32[]{:S(2)}) collective-permute-start(bf16[256,1024]{1,0:T(8,128)(2,1)} %collective-permute-done.5.refs_2_), channel_id=1, source_target_pairs={{0,1},{1,0},{2,3},{3,2},{4,5},{5,4},{6,7},{7,6},{8,9},{9,8},{10,11... | collective-permute-start | bytes 1572872 | tf_op jit(solution)/shard_map/ppermute | solution.py:27
  49.7 7.1 %collective-permute-start.11 = (bf16[256,1024]{1,0:T(8,128)(2,1)}, bf16[256,1024]{1,0:T(8,128)(2,1)}, u32[]{:S(2)}, u32[]{:S(2)}) collective-permute-start(bf16[256,1024]{1,0:T(8,128)(2,1)} %collective-permute-done.6.refs_3_), channel_id=1, source_target_pairs={{0,1},{1,0},{2,3},{3,2},{4,5},{5,4},{6,7},{7,6},{8,9},{9,8},{10,11... | collective-permute-start | bytes 1572872 | tf_op jit(solution)/shard_map/ppermute | solution.py:27
  49.7 90.7 %collective-permute-start.17 = (bf16[512,2048]{1,0:T(8,128)(2,1)S(1)}, bf16[512,2048]{1,0:T(8,128)(2,1)}, u32[]{:S(2)}, u32[]{:S(2)}) collective-permute-start(bf16[512,2048]{1,0:T(8,128)(2,1)S(1)} %multiply_convert_fusion.refs_0_.refs_4_.refs_7_), channel_id=1, source_target_pairs={{0,1},{1,0},{2,3},{3,2},{4,5},{5,4},{6,7},{7,6},{8,9},{9,8},{10,11... | collective-permute-start | bytes 6291464 | tf_op jit(solution)/shard_map/ppermute | solution.py:27
  52.3 77.2 %collective-permute-start.14 = (bf16[512,2048]{1,0:T(8,128)(2,1)S(1)}, bf16[512,2048]{1,0:T(8,128)(2,1)}, u32[]{:S(2)}, u32[]{:S(2)}) collective-permute-start(bf16[512,2048]{1,0:T(8,128)(2,1)S(1)} %multiply_convert_fusion.refs_0_.refs_4_.refs_7_), channel_id=1, source_target_pairs={{2,10},{4,12},{6,14},{10,18},{12,20},{14,22},{18,26},{20,28},{22,3... | collective-permute-start | bytes 6291464 | tf_op jit(solution)/shard_map/ppermute | solution.py:630
  54.3 75.2 %collective-permute-start.12 = (bf16[512,2048]{1,0:T(8,128)(2,1)S(1)}, bf16[512,2048]{1,0:T(8,128)(2,1)S(1)}, u32[]{:S(2)}, u32[]{:S(2)}) collective-permute-start(bf16[512,2048]{1,0:T(8,128)(2,1)S(1)} %multiply_convert_fusion.refs_0_.refs_4_.refs_7_), channel_id=1, source_target_pairs={{0,2},{2,0},{4,6},{6,4},{8,10},{10,8},{12,14},{14,12},{16,18},{18,... | collective-permute-start | bytes 6291464 | tf_op jit(solution)/shard_map/ppermute | solution.py:630
  56.2 73.2 %collective-permute-start.7 = (bf16[512,2048]{1,0:T(8,128)(2,1)S(1)}, bf16[512,2048]{1,0:T(8,128)(2,1)S(1)}, u32[]{:S(2)}, u32[]{:S(2)}) collective-permute-start(bf16[512,2048]{1,0:T(8,128)(2,1)S(1)} %multiply_convert_fusion.refs_0_.refs_4_.refs_7_), channel_id=1, source_target_pairs={{0,4},{2,6},{4,0},{6,2},{8,12},{10,14},{12,8},{14,10},{16,20},{18,... | collective-permute-start | bytes 6291464 | tf_op jit(solution)/shard_map/ppermute | solution.py:630
  129.5 4.9 %copy-start.4 = (bf16[512,2048]{1,0:T(8,128)(2,1)}, bf16[512,2048]{1,0:T(8,128)(2,1)S(1)}, u32[]{:S(2)}) copy-start(bf16[512,2048]{1,0:T(8,128)(2,1)S(1)} %collective-permute-done.12.refs_1_) | copy-start | bytes 6291460
  129.5 4.9 %copy-start.1 = (bf16[512,2048]{1,0:T(8,128)(2,1)}, bf16[512,2048]{1,0:T(8,128)(2,1)S(1)}, u32[]{:S(2)}) copy-start(bf16[512,2048]{1,0:T(8,128)(2,1)S(1)} %collective-permute-done.7.refs_0_) | copy-start | bytes 6291460
  134.4 32.7 %collective-permute-start.16 = (bf16[256,2048]{1,0:T(8,128)(2,1)}, bf16[256,2048]{1,0:T(8,128)(2,1)}, u32[]{:S(2)}, u32[]{:S(2)}) collective-permute-start(bf16[256,2048]{1,0:T(8,128)(2,1)} %get-tuple-element.48), channel_id=1, source_target_pairs={{0,4},{2,6},{4,0},{6,2},{8,12},{10,14},{12,8},{14,10},{16,20},{18,... | collective-permute-start | bytes 3145736 | tf_op jit(solution)/shard_map/ppermute | solution.py:630
  136.0 31.1 %collective-permute-start.15 = (bf16[256,2048]{1,0:T(8,128)(2,1)}, bf16[256,2048]{1,0:T(8,128)(2,1)}, u32[]{:S(2)}, u32[]{:S(2)}) collective-permute-start(bf16[256,2048]{1,0:T(8,128)(2,1)} %get-tuple-element.49), channel_id=1, source_target_pairs={{2,0},{4,6},{6,4},{10,8},{12,14},{14,12},{18,16},{20,22},{22,20},{... | collective-permute-start | bytes 3145736 | tf_op jit(solution)/shard_map/ppermute | solution.py:630
  137.2 29.9 %collective-permute-start.13 = (bf16[256,2048]{1,0:T(8,128)(2,1)}, bf16[256,2048]{1,0:T(8,128)(2,1)S(1)}, u32[]{:S(2)}, u32[]{:S(2)}) collective-permute-start(bf16[256,2048]{1,0:T(8,128)(2,1)} %get-tuple-element.50), channel_id=1, source_target_pairs={{0,8},{2,10},{4,12},{6,14},{8,16},{10,18},{12,20},{14,22},{16,24},... | collective-permute-start | bytes 3145736 | tf_op jit(solution)/shard_map/ppermute | solution.py:630
  140.4 28.0 %copy-start.2 = (bf16[512,2048]{1,0:T(8,128)(2,1)S(1)}, bf16[512,2048]{1,0:T(8,128)(2,1)}, u32[]{:S(2)}) copy-start(bf16[512,2048]{1,0:T(8,128)(2,1)} %copy-done.1) | copy-start | bytes 6291460
  167.1 2.7 %copy-start.3 = (bf16[256,2048]{1,0:T(8,128)(2,1)}, bf16[256,2048]{1,0:T(8,128)(2,1)S(1)}, u32[]{:S(2)}) copy-start(bf16[256,2048]{1,0:T(8,128)(2,1)S(1)} %collective-permute-done.13.refs_2_.refs_1_) | copy-start | bytes 3145732
  167.1 27.3 %collective-permute-start.20 = (bf16[256,2048]{1,0:T(8,128)(2,1)S(1)}, bf16[256,2048]{1,0:T(8,128)(2,1)S(1)}, u32[]{:S(2)}, u32[]{:S(2)}) collective-permute-start(bf16[256,2048]{1,0:T(8,128)(2,1)S(1)} %collective-permute-done.13.refs_2_.refs_1_), channel_id=1, source_target_pairs={{4,0},{6,2},{12,8},{14,10},{20,16},{22,18},{28,24},{30,26},{5,1},{... | collective-permute-start | bytes 3145736 | tf_op jit(solution)/shard_map/ppermute | solution.py:630
  169.9 25.9 %collective-permute-start.19 = (bf16[256,2048]{1,0:T(8,128)(2,1)S(1)}, bf16[256,2048]{1,0:T(8,128)(2,1)S(1)}, u32[]{:S(2)}, u32[]{:S(2)}) collective-permute-start(bf16[256,2048]{1,0:T(8,128)(2,1)S(1)} %get-tuple-element.46), channel_id=1, source_target_pairs={{0,2},{2,0},{6,4},{8,10},{10,8},{14,12},{16,18},{18,16},{22,20},{2... | collective-permute-start | bytes 3145736 | tf_op jit(solution)/shard_map/ppermute | solution.py:630
  174.2 26.8 %collective-permute-start.18 = (bf16[256,2048]{1,0:T(8,128)(2,1)S(1)}, bf16[256,2048]{1,0:T(8,128)(2,1)S(1)}, u32[]{:S(2)}, u32[]{:S(2)}) collective-permute-start(bf16[256,2048]{1,0:T(8,128)(2,1)S(1)} %get-tuple-element.47), channel_id=1, source_target_pairs={{0,8},{8,16},{16,24},{24,0},{1,9},{9,17},{17,25},{25,1}} | collective-permute-start | bytes 3145736 | tf_op jit(solution)/shard_map/ppermute | solution.py:630
  194.4 6.5 %copy-start.5 = (bf16[256,2048]{1,0:T(8,128)(2,1)}, bf16[256,2048]{1,0:T(8,128)(2,1)S(1)}, u32[]{:S(2)}) copy-start(bf16[256,2048]{1,0:T(8,128)(2,1)S(1)} %collective-permute-done.20.refs_6_) | copy-start | bytes 3145732
  195.8 5.2 %copy-start.6 = (bf16[256,2048]{1,0:T(8,128)(2,1)}, bf16[256,2048]{1,0:T(8,128)(2,1)S(1)}, u32[]{:S(2)}) copy-start(bf16[256,2048]{1,0:T(8,128)(2,1)S(1)} %collective-permute-done.19.refs_4_) | copy-start | bytes 3145732
  201.0 1.0 copy-start.7

commit v2 on v1

--- a/solution.py
+++ b/solution.py
@@ -12,7 +12,6 @@
 LAYER = 4
 BLOCK = 128
 GROUP = 8
-BAND = 32
 CHUNK = 256
 VMEM_BYTES = 56 * 1024 * 1024
 
@@ -39,7 +38,10 @@
 
 def dot3(left, right, dims):
     (lh, ll), (rh, rl) = left, right
-    return dot(lh, rh, dims) + (dot(lh, rl, dims) + dot(ll, rh, dims))
+    (left_dim,), (right_dim,) = dims[0]
+    left = jnp.concatenate([lh, ll, lh], axis=left_dim)
+    right = jnp.concatenate([rh, rh, rl], axis=right_dim)
+    return dot(left, right, dims)
 
 
 def half_squares(block):
@@ -125,10 +127,7 @@
         cell = {(a, b): line(cols[b], a) for b in range(GROUP) for a in range(b + 1)}
         held = jnp.where(inside, jnp.where(lane == start + sub, 1.0, 0.0), rows[m])
         lines = [line(held, j) for j in range(GROUP)]
-        band_end = (m * GROUP // BAND + 1) * BAND
-        last = (m + 1) * GROUP == band_end
-        if start % BAND == 0:
-            band = []
+        last = m + 1 == count
         if not last:
             near = [column(rows[m + 1], start + b) for b in range(GROUP)]
             change = None
@@ -163,10 +162,9 @@
             pivots += [top, det * top_inverse]
         done = pick(at, scaled_lines) * lax.rsqrt(pick(at, pivots))
         store(m, jnp.where(lane < start + GROUP, done, 0.0))
-        band.append(jnp.where((lane >= start + GROUP) & (lane < band_end), 0.0, done))
         if not last:
             rows[m + 1] = jnp.where(inside, 0.0, rows[m + 1]) - change
-            others = range(m + 2, band_end // GROUP)
+            others = range(m + 2, count)
             for j in range(GROUP - 4, -1, -2) if len(others) > 0 else ():
                 for b in range(j + 2, GROUP):
                     solved_lines[j] = solved_lines[j] - factors[j, b] * solved_lines[b]
@@ -176,15 +174,6 @@
                 while len(terms) > 1:
                     terms = [a + b for a, b in zip(terms[0::2], terms[1::2])]
                 rows[i] = jnp.where(inside, 0.0, rows[i]) - terms[0]
-        elif m + 1 < count:
-            finished = split(jnp.concatenate(band, axis=0))
-            held_out = (lane >= band_end - BAND) & (lane < band_end)
-            rest = [jnp.where(held_out, rows[i], 0.0) for i in range(m + 1, count)]
-            factor = dot3(split(jnp.concatenate(rest, axis=0)), finished, NT)
-            change = dot3(split(factor), finished, NN)
-            for i in range(m + 1, count):
-                first = GROUP * (i - m - 1)
-                rows[i] = jnp.where(held_out, 0.0, rows[i]) - change[first : first + GROUP, :]
 
 
 def lower_kernel(cols, layers, share, place_ref, *refs):
@@ -192,10 +181,12 @@
     extra_ref, high_ref, low_ref, sq_ref, panel_ref = refs[cols * LAYER : cols * LAYER + 5]
     panel, work, ahead, inv, inv_high, inv_low, sq_col, sems, panel_sem = refs[cols * LAYER + 5 :]
     size = work.shape[0]
-    row = place_ref[0]
+    row, col = place_ref[0], place_ref[1]
     layer, spot = lax.div(row, LAYER), lax.rem(row, LAYER)
+    width = panel.shape[1] // cols
     copies = []
     for e in range(cols):
+        lanes = pl.ds(pl.multiple_of(lax.rem(col - e + cols, cols) * width, width), width)
         for d in range(LAYER):
             for back in range(layers):
                 from_spot = spot + d - 2 * jnp.bitwise_and(spot, d)
@@ -204,7 +195,7 @@
                 copies.append(
                     fetched(
                         pieces[e * LAYER + d].at[back * share : (back + 1) * share, :],
-                        panel.at[e, there, :],
+                        panel.at[there, lanes],
                         sems.at[len(copies)],
                     )
                 )
@@ -214,16 +205,11 @@
     tile = CHUNK
     for r in range(size // tile):
         rows = slice(r * tile, (r + 1) * tile)
-        total = half_squares(panel[0, rows, :])
-        for e in range(1, cols):
-            total = total + half_squares(panel[e, rows, :])
-        sq_col[rows, :] = jnp.broadcast_to(total, (tile, 128))
+        sq_col[rows, :] = jnp.broadcast_to(half_squares(panel[rows, :]), (tile, 128))
     sq_ref[...] = jnp.transpose(sq_col[...])[0:8, :]
     for r in range(size // tile):
         rows = slice(r * tile, (r + 1) * tile)
-        inner = dot(panel[0, rows, :], panel[0], NT)
-        for e in range(1, cols):
-            inner = inner + dot(panel[e, rows, :], panel[e], NT)
+        inner = dot(panel[rows, :], panel[...], NT)
         block = jnp.exp(inner - sq_col[rows, 0:1] - sq_ref[0:1, :])
         on_diagonal = iota((tile, size), 0) + r * tile == iota((tile, size), 1)
         work[rows, :] = block + jnp.where(on_diagonal, extra_ref[...], 0.0)
@@ -261,14 +247,13 @@
         diagonal = ahead[...]
         inverse = (inv_high[...], inv_low[...])
         line = finish_line(k - 1)
-        inside = lax.shift_right_logical(iota((1, size), 1), 7) == k - 1
         for d in range(steps - 1):
             there = place_of(lax.rem(k + d, steps))
             valid = k + d < steps
             factor = dot3(split(work[there, here]), inverse, NT)
             factor = split(jnp.where(valid, factor, 0.0))
-            keep = jnp.where(inside & valid, 0.0, 1.0)
-            work[there, :] = work[there, :] * keep - dot3(factor, line, NN)
+            work[there, here] = jnp.where(valid, 0.0, work[there, here])
+            work[there, :] = work[there, :] - dot3(factor, line, NN)
         factor_block(diagonal, store)
         look_ahead(k)
         return carry
@@ -296,12 +281,12 @@
             jax.ShapeDtypeStruct((size, size), BF16),
             jax.ShapeDtypeStruct((size, size), BF16),
             jax.ShapeDtypeStruct((8, size), F32),
-            jax.ShapeDtypeStruct((cols, size, width), BF16),
+            jax.ShapeDtypeStruct((size, cols * width), BF16),
         ),
         in_specs=[pl.BlockSpec(memory_space=pltpu.SMEM)] + [anywhere] * len(flat) + [vmem],
         out_specs=(vmem, vmem, vmem, anywhere),
         scratch_shapes=[
-            pltpu.VMEM((cols, size, width), BF16),
+            pltpu.VMEM((size, cols * width), BF16),
             pltpu.VMEM((size, size), F32),
             pltpu.VMEM((BLOCK, BLOCK), F32),
             pltpu.VMEM((BLOCK, BLOCK), F32),
@@ -331,20 +316,13 @@
     return jnp.concatenate(parts, axis=1)
 
 
-def panel_rows(x_ref, rows, panel, features, half, sq_row):
-    inner = None
-    width = panel.shape[2]
-    for e, start in enumerate(features):
-        lanes = pl.ds(pl.multiple_of(start * width, width), width)
-        part = dot(x_ref[rows, lanes], panel[e], NT)
-        inner = part if inner is None else inner + part
-    return jnp.exp(inner - half - sq_row)
-
-
-def panel_hits(values, first_local, row, share, extra_ref):
-    local = iota(values.shape, 0) + first_local
-    hit = (local + row * share == iota(values.shape, 1)) & (local < share)
-    return values + jnp.where(hit, extra_ref[...], 0.0)
+def panel_rows(x, panel, half, sq_row, first_local, row, share, extra_ref):
+    block = jnp.exp(dot(x, panel[...], NT) - half - sq_row)
+    top = block[:share, :]
+    local = iota(top.shape, 0) + first_local
+    hit = (local + row * share == iota(top.shape, 1)) & (local < share)
+    top = top + jnp.where(hit, extra_ref[...], 0.0)
+    return jnp.concatenate([top, block[share:, :]], axis=0)
 
 
 def own_kernel(cols, share, place_ref, *refs):
@@ -355,8 +333,6 @@
     row, col = place_ref[0], place_ref[1]
     count = held.shape[0] // cols
     chunk = min(CHUNK, count)
-    places = [lax.rem(col - d + cols, cols) for d in range(cols)]
-    starts = [pl.multiple_of(place * count, count) for place in places]
 
     copies = [fetched(slices[0], held.at[0:count, :], sems.at[0])]
     copies.append(fetched(panel_hbm, panel, sems.at[1]))
@@ -365,7 +341,7 @@
         copies.append(fetched(slices[d], held.at[d * count : (d + 1) * count, :], sems.at[3 + d]))
     per = count // chunk
     block_rows = cols * count
-    for copy in copies[:2] + copies[4:]:
+    for copy in copies:
         copy.wait()
     sq_row = sq_ref[0:1, :]
 
@@ -373,32 +349,28 @@
         place = lax.rem(col - lax.div(r, per) + cols, cols)
         return pl.multiple_of(place * count + lax.rem(r, per) * chunk, chunk)
 
-    def rows_step(r, carry):
-        rows = pl.ds(pl.multiple_of(r * chunk, chunk), chunk)
-        first = first_row(r)
-        there = pl.ds(first, chunk)
-        half = half_squares(held[rows, :])
-        half_ref[there, :] = jnp.broadcast_to(half, (chunk, 128))
-        block = panel_rows(held, rows, panel, places, half, sq_row)
-        block = panel_hits(block, first, row, share, panel_extra_ref)
-
-        @pl.when(r == 0)
-        def _():
-            copies[2].wait()
-            copies[3].wait()
-
-        values = solved(block, high, low)
-        factor[rows, :] = values
-        block_high[there, :], block_low[there, :] = split(values)
+    def rows_step(d, carry):
+        for i in range(per):
+            r = d * per + i
+            rows = pl.ds(pl.multiple_of(r * chunk, chunk), chunk)
+            first = first_row(r)
+            there = pl.ds(first, chunk)
+            x = held[rows, :]
+            half = half_squares(x)
+            half_ref[there, :] = jnp.broadcast_to(half, (chunk, 128))
+            block = panel_rows(x, panel, half, sq_row, first, row, share, panel_extra_ref)
+            values = solved(block, high, low)
+            factor[rows, :] = values
+            block_high[there, :], block_low[there, :] = split(values)
         return carry
 
-    lax.fori_loop(0, cols * per, rows_step, 0)
+    lax.fori_loop(0, cols, rows_step, 0)
     outs = [
         fetched(factor.at[0:count, :], factor_hbm, sems.at[4 + cols]),
         fetched(block_high, block_high_hbm, sems.at[5 + cols]),
         fetched(block_low, block_low_hbm, sems.at[6 + cols]),
     ]
-    mine = pl.ds(starts[0], count)
+    mine = pl.ds(pl.multiple_of(col * count, count), count)
     own_row = as_row(half_ref[mine, 0:1])
 
     def tile_step(r, carry):
@@ -470,7 +442,6 @@
     spot = lax.rem(row, LAYER)
     count = seen.shape[1]
     chunk = min(CHUNK, count)
-    places = [lax.rem(col - d + cols, cols) for d in range(cols)]
     visits = len(routes)
 
     def arrive(v):
@@ -524,27 +495,21 @@
         target = out_hbm.at[:, pl.ds(first, count)]
         return pltpu.make_async_copy(tiles.at[v], target, sems.at[visits + 5 + cols + v])
 
-    loads[0].wait()
+    for load in loads[:3]:
+        load.wait()
 
     def visit_step(v, carry):
         visit_row = lax.rem(row - stop_of(v) + row_count, row_count)
         arrived(v)
         visit_half[...] = jnp.broadcast_to(half_squares(seen[v]), (count, 128))
 
-        def rows_step(r, carry):
-            rows = pl.ds(pl.multiple_of(r * chunk, chunk), chunk)
-            block = panel_rows(seen.at[v], rows, panel, places, visit_half[rows, 0:1], sq_row)
-            block = panel_hits(block, col * count + r * chunk, visit_row, share, panel_extra_ref)
-
-            @pl.when((v == 0) & (r == 0))
-            def _():
-                loads[1].wait()
-                loads[2].wait()
-
+        for r in range(per):
+            rows = slice(r * chunk, (r + 1) * chunk)
+            first = col * count + r * chunk
+            half = visit_half[rows, 0:1]
+            x = seen[v, rows, :]
+            block = panel_rows(x, panel, half, sq_row, first, visit_row, share, panel_extra_ref)
             seen_high[rows, :], seen_low[rows, :] = split(solved(block, high, low))
-            return carry
-
-        lax.fori_loop(0, per, rows_step, 0)
 
         @pl.when(v == 0)
         def _():

time: 234 us -> 205 us (0.88)
  Pallas kernels: 155 us -> 126 us
    pallas_call x1, Pallas kernels: 72.7 us -> 49.3 us  [inverse_lower(): pl.pallas_call(functools.partial(lower_kernel, cols, layers, share), out_...]
    pallas_call x1, Pallas kernels: 26.7 us -> 23.4 us  [own_rows(): pl.pallas_call(functools.partial(own_kernel, cols, share), out_shape=(jax...]
    pallas_call x2, Pallas kernels: 49.3 us -> 46.4 us  [visit(): pl.pallas_call(functools.partial(visit_kernel, cols, share, routes), out_...]
  transfers between devices with their start and end apart: 21 -> 21, of which waited for: 7 -> 7; matrix products, arithmetic and copies ran while one was open for 5% -> 6% of each run, Pallas kernels for 53% -> 47%
where the time goes in v2:
time: 205 us; the launch traced here: 204 us
  Pallas kernels  126 us (61%)
  waiting for transfers between devices  32.8 us (16%)
  starting transfers between devices  29.9 us (15%)
  other arithmetic  9.99 us (5%)
  local copies, waits for them, and re-layouts  4.78 us (2%)
    pallas_call x1, Pallas kernels, inverse_lower(): pl.pallas_call(functools.partial(lower_kernel, cols, layers, share), out_...  49.3 us
    pallas_call x2, Pallas kernels, visit(): pl.pallas_call(functools.partial(visit_kernel, cols, share, routes), out_...  46.4 us
    ppermute x15, waiting for transfers between devices, sent(): return lax.ppermute(block, 'row', pairs)  32.5 us
    ppermute x15, starting transfers between devices, sent(): return lax.ppermute(block, 'row', pairs)  26.4 us
    pallas_call x1, Pallas kernels, own_rows(): pl.pallas_call(functools.partial(own_kernel, cols, share), out_shape=(jax...  23.4 us
    pallas_call x1, Pallas kernels, match_extras(): pl.pallas_call(functools.partial(extras_kernel, min(total, 1024)), out_sh...  6.66 us
    select_n x1, other arithmetic, body(): jnp.where(spot == 2, above2[:mid], jnp.where(spot == 3, above2[mid:], bes...  4.87 us
  transfers between devices with their start and end apart: 21, of which 7 were waited for; matrix products, arithmetic and copies ran while one was open for 6% of the time, Pallas kernels for 47%

profile of v2, /device:TPU:0, one launch (start us, length us, event | category | flops | bytes accessed | tf_op | source)
XLA Modules:
  0.0 204.3 jit_solution(6468359700883009872)
XLA Ops:
  0.6 0.9 slice.30
  1.5 2.4 %collective-permute-start = (bf16[64,1024]{1,0:T(8,128)(2,1)S(1)}, bf16[64,1024]{1,0:T(8,128)(2,1)S(1)}, u32[]{:S(2)}, u32[]{:S(2)}) collective-permute-start(bf16[64,1024]{1,0:T(8,128)(2,1)S(1)} %slice.30), channel_id=1, source_target_pairs={{0,1},{2,3},{4,5},{6,7},{8,9},{10,11},{12,13},{14,15},{16,17},{18,... | collective-permute-start | bytes 393224 | tf_op jit(solution)/shard_map/ppermute | solution.py:623
  3.9 0.7 dynamic_slice.6
  4.6 0.3 collective-permute-done
  4.9 1.0 multiply_convert_fusion.1
  5.8 4.5 %collective-permute-start.3 = (bf16[64,1024]{1,0:T(8,128)(2,1)S(1)}, bf16[64,1024]{1,0:T(8,128)(2,1)S(1)}, u32[]{:S(2)}, u32[]{:S(2)}) collective-permute-start(bf16[64,1024]{1,0:T(8,128)(2,1)S(1)} %multiply_convert_fusion.1), channel_id=1, source_target_pairs={{0,24},{2,26},{4,28},{6,30},{8,0},{10,2},{12,4},{14,6},{16,8},{18,... | collective-permute-start | bytes 393224 | tf_op jit(solution)/shard_map/ppermute | solution.py:595
  10.3 0.0 collective-permute-start.2
  10.3 1.0 collective-permute-start.1
  11.4 2.1 %multiply_convert_fusion.refs_0_.refs_4_.refs_7_ = bf16[512,2048]{1,0:T(8,128)(2,1)S(1)} fusion(bf16[512,2048]{1,0:T(8,128)(2,1)} %param.3, f32[2048]{0:T(1024)} %param.4), kind=kLoop, calls=%fused_computation | loop fusion | flops 3145728 | bytes 4202496 | tf_op jit(solution)/shard_map/convert_element_type | solution.py:627
  13.5 0.7 collective-permute-done.3
  14.3 8.1 %collective-permute-done.2 = bf16[64,1024]{1,0:T(8,128)(2,1)S(1)} collective-permute-done((bf16[64,1024]{1,0:T(8,128)(2,1)S(1)}, bf16[64,1024]{1,0:T(8,128)(2,1)S(1)}, u32[]{:S(2)}, u32[]{:S(2)}) %collective-permute-start.2) | collective-permute-done | bytes 131104 | tf_op jit(solution)/shard_map/ppermute | solution.py:595
  22.4 0.0 copy-start.8
  22.4 0.1 collective-permute-start.8
  22.5 2.5 %collective-permute-start.6 = (bf16[256,1024]{1,0:T(8,128)(2,1)S(1)}, bf16[256,1024]{1,0:T(8,128)(2,1)}, u32[]{:S(2)}, u32[]{:S(2)}) collective-permute-start(bf16[256,1024]{1,0:T(8,128)(2,1)S(1)} %pad_maximum_fusion.refs_0_), channel_id=1, source_target_pairs={{0,6},{2,4},{4,2},{6,0},{8,14},{10,12},{12,10},{14,8},{16,22},{18,... | collective-permute-start | bytes 1572872 | tf_op jit(solution)/shard_map/ppermute | solution.py:595
  25.0 0.5 collective-permute-start.5
  25.5 0.5 collective-permute-start.4
  26.0 6.7 %match_extras.1 = f32[128,128]{1,0:T(8,128)} custom-call(s32[2,16384]{1,0:T(2,128)} %bitcast.3), custom_call_target="tpu_custom_call" | custom-call | flops 8000000000 | bytes 131072 | tf_op jit(solution)/shard_map/match_extras/pallas_call | solution.py:90
  32.7 5.6 %collective-permute-done.6.refs_3_ = bf16[256,1024]{1,0:T(8,128)(2,1)} collective-permute-done((bf16[256,1024]{1,0:T(8,128)(2,1)S(1)}, bf16[256,1024]{1,0:T(8,128)(2,1)}, u32[]{:S(2)}, u32[]{:S(2)}) %collective-permute-start.6) | collective-permute-done | bytes 524320 | tf_op jit(solution)/shard_map/ppermute | solution.py:595
  38.3 10.8 %collective-permute-done.4.refs_1_ = bf16[256,1024]{1,0:T(8,128)(2,1)} collective-permute-done((bf16[256,1024]{1,0:T(8,128)(2,1)S(1)}, bf16[256,1024]{1,0:T(8,128)(2,1)}, u32[]{:S(2)}, u32[]{:S(2)}) %collective-permute-start.4) | collective-permute-done | bytes 524320 | tf_op jit(solution)/shard_map/ppermute | solution.py:595
  49.1 0.0 collective-permute-start.9
  49.1 0.0 collective-permute-done.5.refs_2_
  49.1 0.5 collective-permute-start.10
  49.7 0.0 collective-permute-start.11
  49.7 0.5 collective-permute-start.17
  50.2 0.6 pad_add_fusion.place_ref
  50.7 0.9 reshape.12
  51.6 0.7 reshape.13.refs_8_.refs_6_.refs_13_.refs_16_
  52.3 2.0 collective-permute-start.14
  54.3 0.0 collective-permute-done.9.refs_5_
  54.3 2.0 collective-permute-start.12
  56.2 0.0 collective-permute-done.10.refs_6_
  56.2 0.5 collective-permute-start.7
  56.8 49.3 %inverse_lower.1 = (bf16[1024,1024]{1,0:T(8,128)(2,1)}, bf16[1024,1024]{1,0:T(8,128)(2,1)}, f32[8,1024]{1,0:T(8,128)}, bf16[1024,2048]{1,0:T(8,128)(2,1)}) custom-call(s32[2]{0:T(128)} %pad_add_fusion.place_ref, bf16[256,1024]{1,0:T(8,128)(2,1)} %copy-done.8, bf16[256,1024]{1,0:T(8,128)(2,1)} %collective-permute-done.4.refs_1_, ...), custom_call_target="tpu_custom_call" | custom-call | flops 49999998976 | bytes 8388608 | tf_op jit(solution)/shard_map/inverse_lower/pallas_call | solution.py:278
  106.1 4.9 %select_select_fusion.1 = (bf16[256,2048]{1,0:T(8,128)(2,1)}, bf16[256,2048]{1,0:T(8,128)(2,1)}, bf16[256,2048]{1,0:T(8,128)(2,1)}) fusion(bf16[512,2048]{1,0:T(8,128)(2,1)S(1)} %collective-permute-done.12.refs_1_, bf16[512,2048]{1,0:T(8,128)(2,1)} %collective-permute-done.14, pred[]{:T(512)S(6)} %eq.24, pred[]{:T(512)S(6)} %eq.23, ...), kind=kLoop, calls=%fused_computation.2 | loop fusion | flops 2097152 | bytes 9437187 | tf_op jit(solution)/shard_map/jit(_where)/select_n | solution.py:659
  111.0 1.6 collective-permute-start.16
  112.6 1.3 collective-permute-start.15
  113.9 2.7 %collective-permute-start.13 = (bf16[256,2048]{1,0:T(8,128)(2,1)}, bf16[256,2048]{1,0:T(8,128)(2,1)S(1)}, u32[]{:S(2)}, u32[]{:S(2)}) collective-permute-start(bf16[256,2048]{1,0:T(8,128)(2,1)} %get-tuple-element.50), channel_id=1, source_target_pairs={{0,8},{2,10},{4,12},{6,14},{8,16},{10,18},{12,20},{14,22},{16,24},... | collective-permute-start | bytes 3145736 | tf_op jit(solution)/shard_map/ppermute | solution.py:595
  116.6 0.6 dynamic_slice.7.refs_7_
  117.2 23.4 %own_rows.1 = (f32[1024,2048]{1,0:T(8,128)}, f32[512,1024]{1,0:T(8,128)}, bf16[1024,1024]{1,0:T(8,128)(2,1)}, bf16[1024,1024]{1,0:T(8,128)(2,1)}, f32[1024,128]{1,0:T(8,128)}) custom-call(s32[2]{0:T(128)} %pad_add_fusion.place_ref, bf16[512,2048]{1,0:T(8,128)(2,1)} %copy-done, bf16[512,2048]{1,0:T(8,128)(2,1)} %collective-permute-done.17.refs_1_.refs_5_.refs_8_, ...), custom_call_target="tpu_custom_call" | custom-call | flops 1048576 | bytes 1048576 | tf_op jit(solution)/shard_map/own_rows/pallas_call | solution.py:399
  140.7 1.3 collective-permute-start.20
  142.0 1.4 select_select_fusion
  143.4 4.1 %collective-permute-start.19 = (bf16[256,2048]{1,0:T(8,128)(2,1)S(1)}, bf16[256,2048]{1,0:T(8,128)(2,1)S(1)}, u32[]{:S(2)}, u32[]{:S(2)}) collective-permute-start(bf16[256,2048]{1,0:T(8,128)(2,1)S(1)} %get-tuple-element.46), channel_id=1, source_target_pairs={{0,2},{2,0},{6,4},{8,10},{10,8},{14,12},{16,18},{18,16},{22,20},{2... | collective-permute-start | bytes 3145736 | tf_op jit(solution)/shard_map/ppermute | solution.py:595
  147.5 1.9 collective-permute-start.18
  149.5 17.6 %visit_first.1.refs_17_ = f32[1024,2048]{1,0:T(8,128)} custom-call(s32[2]{0:T(128)} %pad_add_fusion.place_ref, bf16[512,2048]{1,0:T(8,128)(2,1)} %copy-done.1, bf16[512,2048]{1,0:T(8,128)(2,1)} %copy-done.4, bf16[256,2048]{1,0:T(8,128)(2,1)} %copy-done.3, bf16[256,2048]{1,0:T(8,128)(2,1)} %collective-permute-done.15.refs_3_, ...), custom_call_target="tpu_custom_call", output_to_operand_aliasing={{}: (15, {})} | custom-call | flops 524288 | bytes 524288 | tf_op jit(solution)/shard_map/visit_first/pallas_call | solution.py:550
  167.1 2.0 %collective-permute-done.19.refs_4_ = bf16[256,2048]{1,0:T(8,128)(2,1)S(1)} collective-permute-done((bf16[256,2048]{1,0:T(8,128)(2,1)S(1)}, bf16[256,2048]{1,0:T(8,128)(2,1)S(1)}, u32[]{:S(2)}, u32[]{:S(2)}) %collective-permute-start.19) | collective-permute-done | bytes 1048608 | tf_op jit(solution)/shard_map/ppermute | solution.py:595
  169.2 5.2 %collective-permute-done.18.refs_2_ = bf16[256,2048]{1,0:T(8,128)(2,1)S(1)} collective-permute-done((bf16[256,2048]{1,0:T(8,128)(2,1)S(1)}, bf16[256,2048]{1,0:T(8,128)(2,1)S(1)}, u32[]{:S(2)}, u32[]{:S(2)}) %collective-permute-start.18) | collective-permute-done | bytes 1048608 | tf_op jit(solution)/shard_map/ppermute | solution.py:595
  174.3 1.0 copy-done.7
  175.3 28.8 %visit_rest.1 = f32[1024,2048]{1,0:T(8,128)} custom-call(s32[2]{0:T(128)} %pad_add_fusion.place_ref, bf16[512,2048]{1,0:T(8,128)(2,1)} %copy-done.1, bf16[256,2048]{1,0:T(8,128)(2,1)} %copy-done.3, bf16[256,2048]{1,0:T(8,128)(2,1)} %copy-done.7, bf16[256,2048]{1,0:T(8,128)(2,1)} %collective-permute-done.15.refs_3_, ...), custom_call_target="tpu_custom_call", output_to_operand_aliasing={{}: (18, {})} | custom-call | flops 524288 | bytes 524288 | tf_op jit(solution)/shard_map/visit_rest/pallas_call | solution.py:550
  (29 shorter events, 0.1 us)
Async XLA Ops:
  1.5 3.3 %collective-permute-start = (bf16[64,1024]{1,0:T(8,128)(2,1)S(1)}, bf16[64,1024]{1,0:T(8,128)(2,1)S(1)}, u32[]{:S(2)}, u32[]{:S(2)}) collective-permute-start(bf16[64,1024]{1,0:T(8,128)(2,1)S(1)} %slice.30), channel_id=1, source_target_pairs={{0,1},{2,3},{4,5},{6,7},{8,9},{10,11},{12,13},{14,15},{16,17},{18,... | collective-permute-start | bytes 393224 | tf_op jit(solution)/shard_map/ppermute | solution.py:623
  5.8 8.4 %collective-permute-start.3 = (bf16[64,1024]{1,0:T(8,128)(2,1)S(1)}, bf16[64,1024]{1,0:T(8,128)(2,1)S(1)}, u32[]{:S(2)}, u32[]{:S(2)}) collective-permute-start(bf16[64,1024]{1,0:T(8,128)(2,1)S(1)} %multiply_convert_fusion.1), channel_id=1, source_target_pairs={{0,24},{2,26},{4,28},{6,30},{8,0},{10,2},{12,4},{14,6},{16,8},{18,... | collective-permute-start | bytes 393224 | tf_op jit(solution)/shard_map/ppermute | solution.py:595
  10.3 12.0 %collective-permute-start.2 = (bf16[64,1024]{1,0:T(8,128)(2,1)S(1)}, bf16[64,1024]{1,0:T(8,128)(2,1)S(1)}, u32[]{:S(2)}, u32[]{:S(2)}) collective-permute-start(bf16[64,1024]{1,0:T(8,128)(2,1)S(1)} %multiply_convert_fusion.1), channel_id=1, source_target_pairs={{0,16},{2,18},{4,20},{6,22},{8,24},{10,26},{12,28},{14,30},{16,0},... | collective-permute-start | bytes 393224 | tf_op jit(solution)/shard_map/ppermute | solution.py:595
  10.3 12.0 %collective-permute-start.1 = (bf16[64,1024]{1,0:T(8,128)(2,1)S(1)}, bf16[64,1024]{1,0:T(8,128)(2,1)S(1)}, u32[]{:S(2)}, u32[]{:S(2)}) collective-permute-start(bf16[64,1024]{1,0:T(8,128)(2,1)S(1)} %multiply_convert_fusion.1), channel_id=1, source_target_pairs={{0,8},{2,10},{4,12},{6,14},{8,16},{10,18},{12,20},{14,22},{16,24},... | collective-permute-start | bytes 393224 | tf_op jit(solution)/shard_map/ppermute | solution.py:595
  13.5 42.7 %copy-start = (bf16[512,2048]{1,0:T(8,128)(2,1)}, bf16[512,2048]{1,0:T(8,128)(2,1)S(1)}, u32[]{:S(2)}) copy-start(bf16[512,2048]{1,0:T(8,128)(2,1)S(1)} %multiply_convert_fusion.refs_0_.refs_4_.refs_7_) | copy-start | bytes 6291460
  22.4 10.3 %copy-start.8 = (bf16[256,1024]{1,0:T(8,128)(2,1)}, bf16[256,1024]{1,0:T(8,128)(2,1)S(1)}, u32[]{:S(2)}) copy-start(bf16[256,1024]{1,0:T(8,128)(2,1)S(1)} %pad_maximum_fusion.refs_0_) | copy-start | bytes 1572868
  22.4 29.9 %collective-permute-start.8 = (bf16[256,1024]{1,0:T(8,128)(2,1)S(1)}, bf16[256,1024]{1,0:T(8,128)(2,1)}, u32[]{:S(2)}, u32[]{:S(2)}) collective-permute-start(bf16[256,1024]{1,0:T(8,128)(2,1)S(1)} %pad_maximum_fusion.refs_0_), channel_id=1, source_target_pairs={{0,1},{1,0},{2,3},{3,2},{4,5},{5,4},{6,7},{7,6},{8,9},{9,8},{10,11... | collective-permute-start | bytes 1572872 | tf_op jit(solution)/shard_map/ppermute | solution.py:26
  22.5 15.8 %collective-permute-start.6 = (bf16[256,1024]{1,0:T(8,128)(2,1)S(1)}, bf16[256,1024]{1,0:T(8,128)(2,1)}, u32[]{:S(2)}, u32[]{:S(2)}) collective-permute-start(bf16[256,1024]{1,0:T(8,128)(2,1)S(1)} %pad_maximum_fusion.refs_0_), channel_id=1, source_target_pairs={{0,6},{2,4},{4,2},{6,0},{8,14},{10,12},{12,10},{14,8},{16,22},{18,... | collective-permute-start | bytes 1572872 | tf_op jit(solution)/shard_map/ppermute | solution.py:595
  25.0 24.2 %collective-permute-start.5 = (bf16[256,1024]{1,0:T(8,128)(2,1)S(1)}, bf16[256,1024]{1,0:T(8,128)(2,1)}, u32[]{:S(2)}, u32[]{:S(2)}) collective-permute-start(bf16[256,1024]{1,0:T(8,128)(2,1)S(1)} %pad_maximum_fusion.refs_0_), channel_id=1, source_target_pairs={{0,4},{2,6},{4,0},{6,2},{8,12},{10,14},{12,8},{14,10},{16,20},{18,... | collective-permute-start | bytes 1572872 | tf_op jit(solution)/shard_map/ppermute | solution.py:595
  25.5 23.7 %collective-permute-start.4 = (bf16[256,1024]{1,0:T(8,128)(2,1)S(1)}, bf16[256,1024]{1,0:T(8,128)(2,1)}, u32[]{:S(2)}, u32[]{:S(2)}) collective-permute-start(bf16[256,1024]{1,0:T(8,128)(2,1)S(1)} %pad_maximum_fusion.refs_0_), channel_id=1, source_target_pairs={{0,2},{2,0},{4,6},{6,4},{8,10},{10,8},{12,14},{14,12},{16,18},{18,... | collective-permute-start | bytes 1572872 | tf_op jit(solution)/shard_map/ppermute | solution.py:595
  49.1 5.1 %collective-permute-start.9 = (bf16[256,1024]{1,0:T(8,128)(2,1)}, bf16[256,1024]{1,0:T(8,128)(2,1)}, u32[]{:S(2)}, u32[]{:S(2)}) collective-permute-start(bf16[256,1024]{1,0:T(8,128)(2,1)} %collective-permute-done.4.refs_1_), channel_id=1, source_target_pairs={{0,1},{1,0},{2,3},{3,2},{4,5},{5,4},{6,7},{7,6},{8,9},{9,8},{10,11... | collective-permute-start | bytes 1572872 | tf_op jit(solution)/shard_map/ppermute | solution.py:26
  49.1 7.1 %collective-permute-start.10 = (bf16[256,1024]{1,0:T(8,128)(2,1)}, bf16[256,1024]{1,0:T(8,128)(2,1)}, u32[]{:S(2)}, u32[]{:S(2)}) collective-permute-start(bf16[256,1024]{1,0:T(8,128)(2,1)} %collective-permute-done.5.refs_2_), channel_id=1, source_target_pairs={{0,1},{1,0},{2,3},{3,2},{4,5},{5,4},{6,7},{7,6},{8,9},{9,8},{10,11... | collective-permute-start | bytes 1572872 | tf_op jit(solution)/shard_map/ppermute | solution.py:26
  49.7 7.1 %collective-permute-start.11 = (bf16[256,1024]{1,0:T(8,128)(2,1)}, bf16[256,1024]{1,0:T(8,128)(2,1)}, u32[]{:S(2)}, u32[]{:S(2)}) collective-permute-start(bf16[256,1024]{1,0:T(8,128)(2,1)} %collective-permute-done.6.refs_3_), channel_id=1, source_target_pairs={{0,1},{1,0},{2,3},{3,2},{4,5},{5,4},{6,7},{7,6},{8,9},{9,8},{10,11... | collective-permute-start | bytes 1572872 | tf_op jit(solution)/shard_map/ppermute | solution.py:26
  49.7 67.5 %collective-permute-start.17 = (bf16[512,2048]{1,0:T(8,128)(2,1)S(1)}, bf16[512,2048]{1,0:T(8,128)(2,1)}, u32[]{:S(2)}, u32[]{:S(2)}) collective-permute-start(bf16[512,2048]{1,0:T(8,128)(2,1)S(1)} %multiply_convert_fusion.refs_0_.refs_4_.refs_7_), channel_id=1, source_target_pairs={{0,1},{1,0},{2,3},{3,2},{4,5},{5,4},{6,7},{7,6},{8,9},{9,8},{10,11... | collective-permute-start | bytes 6291464 | tf_op jit(solution)/shard_map/ppermute | solution.py:26
  52.3 53.8 %collective-permute-start.14 = (bf16[512,2048]{1,0:T(8,128)(2,1)S(1)}, bf16[512,2048]{1,0:T(8,128)(2,1)}, u32[]{:S(2)}, u32[]{:S(2)}) collective-permute-start(bf16[512,2048]{1,0:T(8,128)(2,1)S(1)} %multiply_convert_fusion.refs_0_.refs_4_.refs_7_), channel_id=1, source_target_pairs={{2,10},{4,12},{6,14},{10,18},{12,20},{14,22},{18,26},{20,28},{22,3... | collective-permute-start | bytes 6291464 | tf_op jit(solution)/shard_map/ppermute | solution.py:595
  54.3 51.8 %collective-permute-start.12 = (bf16[512,2048]{1,0:T(8,128)(2,1)S(1)}, bf16[512,2048]{1,0:T(8,128)(2,1)S(1)}, u32[]{:S(2)}, u32[]{:S(2)}) collective-permute-start(bf16[512,2048]{1,0:T(8,128)(2,1)S(1)} %multiply_convert_fusion.refs_0_.refs_4_.refs_7_), channel_id=1, source_target_pairs={{0,2},{2,0},{4,6},{6,4},{8,10},{10,8},{12,14},{14,12},{16,18},{18,... | collective-permute-start | bytes 6291464 | tf_op jit(solution)/shard_map/ppermute | solution.py:595
  56.2 49.8 %collective-permute-start.7 = (bf16[512,2048]{1,0:T(8,128)(2,1)S(1)}, bf16[512,2048]{1,0:T(8,128)(2,1)S(1)}, u32[]{:S(2)}, u32[]{:S(2)}) collective-permute-start(bf16[512,2048]{1,0:T(8,128)(2,1)S(1)} %multiply_convert_fusion.refs_0_.refs_4_.refs_7_), channel_id=1, source_target_pairs={{0,4},{2,6},{4,0},{6,2},{8,12},{10,14},{12,8},{14,10},{16,20},{18,... | collective-permute-start | bytes 6291464 | tf_op jit(solution)/shard_map/ppermute | solution.py:595
  106.1 4.9 %copy-start.4 = (bf16[512,2048]{1,0:T(8,128)(2,1)}, bf16[512,2048]{1,0:T(8,128)(2,1)S(1)}, u32[]{:S(2)}) copy-start(bf16[512,2048]{1,0:T(8,128)(2,1)S(1)} %collective-permute-done.12.refs_1_) | copy-start | bytes 6291460
  106.1 4.9 %copy-start.1 = (bf16[512,2048]{1,0:T(8,128)(2,1)}, bf16[512,2048]{1,0:T(8,128)(2,1)S(1)}, u32[]{:S(2)}) copy-start(bf16[512,2048]{1,0:T(8,128)(2,1)S(1)} %collective-permute-done.7.refs_0_) | copy-start | bytes 6291460
  111.0 29.7 %collective-permute-start.16 = (bf16[256,2048]{1,0:T(8,128)(2,1)}, bf16[256,2048]{1,0:T(8,128)(2,1)}, u32[]{:S(2)}, u32[]{:S(2)}) collective-permute-start(bf16[256,2048]{1,0:T(8,128)(2,1)} %get-tuple-element.48), channel_id=1, source_target_pairs={{0,4},{2,6},{4,0},{6,2},{8,12},{10,14},{12,8},{14,10},{16,20},{18,... | collective-permute-start | bytes 3145736 | tf_op jit(solution)/shard_map/ppermute | solution.py:595
  112.6 28.1 %collective-permute-start.15 = (bf16[256,2048]{1,0:T(8,128)(2,1)}, bf16[256,2048]{1,0:T(8,128)(2,1)}, u32[]{:S(2)}, u32[]{:S(2)}) collective-permute-start(bf16[256,2048]{1,0:T(8,128)(2,1)} %get-tuple-element.49), channel_id=1, source_target_pairs={{2,0},{4,6},{6,4},{10,8},{12,14},{14,12},{18,16},{20,22},{22,20},{... | collective-permute-start | bytes 3145736 | tf_op jit(solution)/shard_map/ppermute | solution.py:595
  113.9 26.8 %collective-permute-start.13 = (bf16[256,2048]{1,0:T(8,128)(2,1)}, bf16[256,2048]{1,0:T(8,128)(2,1)S(1)}, u32[]{:S(2)}, u32[]{:S(2)}) collective-permute-start(bf16[256,2048]{1,0:T(8,128)(2,1)} %get-tuple-element.50), channel_id=1, source_target_pairs={{0,8},{2,10},{4,12},{6,14},{8,16},{10,18},{12,20},{14,22},{16,24},... | collective-permute-start | bytes 3145736 | tf_op jit(solution)/shard_map/ppermute | solution.py:595
  117.2 24.8 %copy-start.2 = (bf16[512,2048]{1,0:T(8,128)(2,1)S(1)}, bf16[512,2048]{1,0:T(8,128)(2,1)}, u32[]{:S(2)}) copy-start(bf16[512,2048]{1,0:T(8,128)(2,1)} %copy-done.1) | copy-start | bytes 6291460
  140.7 2.7 %copy-start.3 = (bf16[256,2048]{1,0:T(8,128)(2,1)}, bf16[256,2048]{1,0:T(8,128)(2,1)S(1)}, u32[]{:S(2)}) copy-start(bf16[256,2048]{1,0:T(8,128)(2,1)S(1)} %collective-permute-done.13.refs_2_.refs_1_) | copy-start | bytes 3145732
  140.7 26.4 %collective-permute-start.20 = (bf16[256,2048]{1,0:T(8,128)(2,1)S(1)}, bf16[256,2048]{1,0:T(8,128)(2,1)S(1)}, u32[]{:S(2)}, u32[]{:S(2)}) collective-permute-start(bf16[256,2048]{1,0:T(8,128)(2,1)S(1)} %collective-permute-done.13.refs_2_.refs_1_), channel_id=1, source_target_pairs={{4,0},{6,2},{12,8},{14,10},{20,16},{22,18},{28,24},{30,26},{5,1},{... | collective-permute-start | bytes 3145736 | tf_op jit(solution)/shard_map/ppermute | solution.py:595
  143.4 25.7 %collective-permute-start.19 = (bf16[256,2048]{1,0:T(8,128)(2,1)S(1)}, bf16[256,2048]{1,0:T(8,128)(2,1)S(1)}, u32[]{:S(2)}, u32[]{:S(2)}) collective-permute-start(bf16[256,2048]{1,0:T(8,128)(2,1)S(1)} %get-tuple-element.46), channel_id=1, source_target_pairs={{0,2},{2,0},{6,4},{8,10},{10,8},{14,12},{16,18},{18,16},{22,20},{2... | collective-permute-start | bytes 3145736 | tf_op jit(solution)/shard_map/ppermute | solution.py:595
  147.5 26.8 %collective-permute-start.18 = (bf16[256,2048]{1,0:T(8,128)(2,1)S(1)}, bf16[256,2048]{1,0:T(8,128)(2,1)S(1)}, u32[]{:S(2)}, u32[]{:S(2)}) collective-permute-start(bf16[256,2048]{1,0:T(8,128)(2,1)S(1)} %get-tuple-element.47), channel_id=1, source_target_pairs={{0,8},{8,16},{16,24},{24,0},{1,9},{9,17},{17,25},{25,1}} | collective-permute-start | bytes 3145736 | tf_op jit(solution)/shard_map/ppermute | solution.py:595
  167.1 7.2 %copy-start.5 = (bf16[256,2048]{1,0:T(8,128)(2,1)}, bf16[256,2048]{1,0:T(8,128)(2,1)S(1)}, u32[]{:S(2)}) copy-start(bf16[256,2048]{1,0:T(8,128)(2,1)S(1)} %collective-permute-done.20.refs_6_) | copy-start | bytes 3145732
  169.2 5.2 %copy-start.6 = (bf16[256,2048]{1,0:T(8,128)(2,1)}, bf16[256,2048]{1,0:T(8,128)(2,1)S(1)}, u32[]{:S(2)}) copy-start(bf16[256,2048]{1,0:T(8,128)(2,1)S(1)} %collective-permute-done.19.refs_4_) | copy-start | bytes 3145732
  174.3 1.0 copy-start.7

commit v3 on v2

--- a/solution.py
+++ b/solution.py
@@ -12,6 +12,7 @@
 LAYER = 4
 BLOCK = 128
 GROUP = 8
+CUT = 6
 CHUNK = 256
 VMEM_BYTES = 56 * 1024 * 1024
 
@@ -176,10 +177,100 @@
                 rows[i] = jnp.where(inside, 0.0, rows[i]) - terms[0]
 
 
-def lower_kernel(cols, layers, share, place_ref, *refs):
+def elimination(work, ahead, inv, inv_high, inv_low):
+    size = work.shape[0]
+    steps = size // BLOCK
+
+    def place_of(k):
+        return pl.ds(pl.multiple_of(k * BLOCK, BLOCK), BLOCK)
+
+    def store(m, values):
+        inv[GROUP * m : GROUP * (m + 1), :] = values
+
+    def look_ahead(k):
+        here, there = place_of(k), place_of(lax.rem(k + 1, steps))
+        inverse = split(inv[...])
+        inv_high[...], inv_low[...] = inverse
+        factor = split(dot3(split(work[there, here]), inverse, NT))
+        ahead[...] = work[there, there] - dot3(factor, factor, NT)
+
+    def finish_line(k):
+        here = place_of(k)
+        inverse = (inv_high[...], inv_low[...])
+        line = dot3(inverse, split(work[here, :]), NN)
+        inside = lax.shift_right_logical(iota((BLOCK, size), 1), 7) == k
+        whole = inv_high[...].astype(F32) + inv_low[...].astype(F32)
+        line = jnp.where(inside, jnp.concatenate([whole] * steps, axis=1), line)
+        work[here, :] = line
+        return split(line)
+
+    def begin():
+        factor_block(work[0:BLOCK, 0:BLOCK], store)
+        look_ahead(0)
+
+    def eliminate(k, carry):
+        here = place_of(k - 1)
+        diagonal = ahead[...]
+        inverse = (inv_high[...], inv_low[...])
+        line = finish_line(k - 1)
+        for d in range(steps - 1):
+            there = place_of(lax.rem(k + d, steps))
+            valid = k + d < steps
+            factor = dot3(split(work[there, here]), inverse, NT)
+            factor = split(jnp.where(valid, factor, 0.0))
+            work[there, here] = jnp.where(valid, 0.0, work[there, here])
+            work[there, :] = work[there, :] - dot3(factor, line, NN)
+        factor_block(diagonal, store)
+        look_ahead(k)
+        return carry
+
+    return begin, eliminate, finish_line
+
+
+def rest_kernel(work_hbm, ahead_in, inv_high_in, inv_low_in, high_ref, low_ref, *scratch):
+    work, ahead, inv, inv_high, inv_low, sem = scratch
+    fetched(work_hbm, work, sem).wait()
+    ahead[...], inv_high[...], inv_low[...] = ahead_in[...], inv_high_in[...], inv_low_in[...]
+    size = work.shape[0]
+    steps = size // BLOCK
+    _, eliminate, finish_line = elimination(work, ahead, inv, inv_high, inv_low)
+    lax.fori_loop(CUT, steps, eliminate, 0)
+    finish_line(steps - 1)
+    for r in range(steps):
+        rows = slice(r * BLOCK, (r + 1) * BLOCK)
+        kept = iota((BLOCK, size), 0) + r * BLOCK >= iota((BLOCK, size), 1)
+        high_ref[rows, :], low_ref[rows, :] = split(jnp.where(kept, work[rows, :], 0.0))
+
+
+def finish_lower(state):
+    work, ahead, inv_high, inv_low = state
+    size = work.shape[0]
+    vmem = pl.BlockSpec(memory_space=pltpu.VMEM)
+    return pl.pallas_call(
+        rest_kernel,
+        out_shape=(jax.ShapeDtypeStruct((size, size), BF16),) * 2,
+        in_specs=[pl.BlockSpec(memory_space=pl.ANY)] + [vmem] * 3,
+        out_specs=(vmem, vmem),
+        scratch_shapes=[
+            pltpu.VMEM((size, size), F32),
+            pltpu.VMEM((BLOCK, BLOCK), F32),
+            pltpu.VMEM((BLOCK, BLOCK), F32),
+            pltpu.VMEM((BLOCK, BLOCK), BF16),
+            pltpu.VMEM((BLOCK, BLOCK), BF16),
+            pltpu.SemaphoreType.DMA,
+        ],
+        cost_estimate=pl.CostEstimate(flops=size, bytes_accessed=size, transcendentals=0),
+        compiler_params=pltpu.CompilerParams(vmem_limit_bytes=VMEM_BYTES),
+        name="finish_lower",
+    )(work, ahead, inv_high, inv_low)
+
+
+def start_kernel(cols, layers, share, place_ref, *refs):
     pieces = refs[: cols * LAYER]
-    extra_ref, high_ref, low_ref, sq_ref, panel_ref = refs[cols * LAYER : cols * LAYER + 5]
-    panel, work, ahead, inv, inv_high, inv_low, sq_col, sems, panel_sem = refs[cols * LAYER + 5 :]
+    extra_ref, sq_ref, panel_ref, work, ahead, inv_high, inv_low = refs[
+        cols * LAYER : cols * LAYER + 7
+    ]
+    panel, inv, sq_col, sems, panel_sem = refs[cols * LAYER + 7 :]
     size = work.shape[0]
     row, col = place_ref[0], place_ref[1]
     layer, spot = lax.div(row, LAYER), lax.rem(row, LAYER)
@@ -214,60 +305,13 @@
         on_diagonal = iota((tile, size), 0) + r * tile == iota((tile, size), 1)
         work[rows, :] = block + jnp.where(on_diagonal, extra_ref[...], 0.0)
 
-    steps = size // BLOCK
-
-    def place_of(k):
-        return pl.ds(pl.multiple_of(k * BLOCK, BLOCK), BLOCK)
-
-    def store(m, values):
-        inv[GROUP * m : GROUP * (m + 1), :] = values
-
-    def look_ahead(k):
-        here, there = place_of(k), place_of(lax.rem(k + 1, steps))
-        inverse = split(inv[...])
-        inv_high[...], inv_low[...] = inverse
-        factor = split(dot3(split(work[there, here]), inverse, NT))
-        ahead[...] = work[there, there] - dot3(factor, factor, NT)
-
-    def finish_line(k):
-        here = place_of(k)
-        inverse = (inv_high[...], inv_low[...])
-        line = dot3(inverse, split(work[here, :]), NN)
-        inside = lax.shift_right_logical(iota((BLOCK, size), 1), 7) == k
-        whole = inv_high[...].astype(F32) + inv_low[...].astype(F32)
-        line = jnp.where(inside, jnp.concatenate([whole] * steps, axis=1), line)
-        work[here, :] = line
-        return split(line)
-
-    factor_block(work[0:BLOCK, 0:BLOCK], store)
-    look_ahead(0)
-
-    def eliminate(k, carry):
-        here = place_of(k - 1)
-        diagonal = ahead[...]
-        inverse = (inv_high[...], inv_low[...])
-        line = finish_line(k - 1)
-        for d in range(steps - 1):
-            there = place_of(lax.rem(k + d, steps))
-            valid = k + d < steps
-            factor = dot3(split(work[there, here]), inverse, NT)
-            factor = split(jnp.where(valid, factor, 0.0))
-            work[there, here] = jnp.where(valid, 0.0, work[there, here])
-            work[there, :] = work[there, :] - dot3(factor, line, NN)
-        factor_block(diagonal, store)
-        look_ahead(k)
-        return carry
-
-    lax.fori_loop(1, steps, eliminate, 0)
-    finish_line(steps - 1)
-    for r in range(steps):
-        rows = slice(r * BLOCK, (r + 1) * BLOCK)
-        kept = iota((BLOCK, size), 0) + r * BLOCK >= iota((BLOCK, size), 1)
-        high_ref[rows, :], low_ref[rows, :] = split(jnp.where(kept, work[rows, :], 0.0))
+    begin, eliminate, _ = elimination(work, ahead, inv, inv_high, inv_low)
+    begin()
+    lax.fori_loop(1, CUT, eliminate, 0)
     saved.wait()
 
 
-def inverse_lower(place, pieces, panel_extra, share):
+def start_lower(place, pieces, panel_extra, share):
     size = panel_extra.shape[1]
     cols = len(pieces)
     held, width = pieces[0][0].shape
@@ -276,22 +320,20 @@
     vmem = pl.BlockSpec(memory_space=pltpu.VMEM)
     anywhere = pl.BlockSpec(memory_space=pl.ANY)
     return pl.pallas_call(
-        functools.partial(lower_kernel, cols, layers, share),
+        functools.partial(start_kernel, cols, layers, share),
         out_shape=(
-            jax.ShapeDtypeStruct((size, size), BF16),
-            jax.ShapeDtypeStruct((size, size), BF16),
             jax.ShapeDtypeStruct((8, size), F32),
             jax.ShapeDtypeStruct((size, cols * width), BF16),
+            jax.ShapeDtypeStruct((size, size), F32),
+            jax.ShapeDtypeStruct((BLOCK, BLOCK), F32),
+            jax.ShapeDtypeStruct((BLOCK, BLOCK), BF16),
+            jax.ShapeDtypeStruct((BLOCK, BLOCK), BF16),
         ),
         in_specs=[pl.BlockSpec(memory_space=pltpu.SMEM)] + [anywhere] * len(flat) + [vmem],
-        out_specs=(vmem, vmem, vmem, anywhere),
+        out_specs=(vmem, anywhere, vmem, vmem, vmem, vmem),
         scratch_shapes=[
             pltpu.VMEM((size, cols * width), BF16),
-            pltpu.VMEM((size, size), F32),
             pltpu.VMEM((BLOCK, BLOCK), F32),
-            pltpu.VMEM((BLOCK, BLOCK), F32),
-            pltpu.VMEM((BLOCK, BLOCK), BF16),
-            pltpu.VMEM((BLOCK, BLOCK), BF16),
             pltpu.VMEM((size, 128), F32),
             pltpu.SemaphoreType.DMA((cols * LAYER * layers,)),
             pltpu.SemaphoreType.DMA,
@@ -300,29 +342,41 @@
             flops=50_000_000_000, bytes_accessed=8 * size * size, transcendentals=size * size
         ),
         compiler_params=pltpu.CompilerParams(vmem_limit_bytes=VMEM_BYTES),
-        name="inverse_lower",
+        name="start_lower",
     )(place, *flat, panel_extra)
 
 
-def solved(values, high_ref, low_ref):
-    high, low = split(values)
-    size = high.shape[1]
-    parts = []
+def factor_rows(x, panel, half, sq_row, first_local, row, share, extra_ref, inverse):
+    size = panel.shape[0]
+    high_ref, low_ref = inverse
+
+    def inner(j):
+        return dot(x, panel[CHUNK * j : CHUNK * (j + 1), :], NT)
+
+    def kernel_tile(j, products):
+        lanes = slice(CHUNK * j, CHUNK * (j + 1))
+        tile = jnp.exp(products - half - sq_row[:, lanes])
+        top = tile[:share, :]
+        local = iota(top.shape, 0) + first_local
+        hit = (local + row * share == iota(top.shape, 1) + CHUNK * j) & (local < share)
+        top = top + jnp.where(hit, extra_ref[:, lanes], 0.0)
+        return split(jnp.concatenate([top, tile[share:, :]], axis=0))
+
+    highs, lows, parts = [], [], []
+    products = inner(0)
     for j in range(size // CHUNK):
-        upto = CHUNK * (j + 1)
-        rows = slice(CHUNK * j, upto)
-        inverse = (high_ref[rows, :upto], low_ref[rows, :upto])
-        parts.append(dot3((high[:, :upto], low[:, :upto]), inverse, NT))
+        current = products
+        if CHUNK * (j + 1) < size:
+            products = inner(j + 1)
+        high, low = kernel_tile(j, current)
+        highs.append(high)
+        lows.append(low)
+        rows, upto = slice(CHUNK * j, CHUNK * (j + 1)), CHUNK * (j + 1)
+        left = jnp.concatenate(highs + lows + highs, axis=1)
+        inv_high, inv_low = high_ref[rows, :upto], low_ref[rows, :upto]
+        right = jnp.concatenate([inv_high, inv_high, inv_low], axis=1)
+        parts.append(dot(left, right, NT))
     return jnp.concatenate(parts, axis=1)
-
-
-def panel_rows(x, panel, half, sq_row, first_local, row, share, extra_ref):
-    block = jnp.exp(dot(x, panel[...], NT) - half - sq_row)
-    top = block[:share, :]
-    local = iota(top.shape, 0) + first_local
-    hit = (local + row * share == iota(top.shape, 1)) & (local < share)
-    top = top + jnp.where(hit, extra_ref[...], 0.0)
-    return jnp.concatenate([top, block[share:, :]], axis=0)
 
 
 def own_kernel(cols, share, place_ref, *refs):
@@ -358,8 +412,9 @@
             x = held[rows, :]
             half = half_squares(x)
             half_ref[there, :] = jnp.broadcast_to(half, (chunk, 128))
-            block = panel_rows(x, panel, half, sq_row, first, row, share, panel_extra_ref)
-            values = solved(block, high, low)
+            values = factor_rows(
+                x, panel, half, sq_row, first, row, share, panel_extra_ref, (high, low)
+            )
             factor[rows, :] = values
             block_high[there, :], block_low[there, :] = split(values)
         return carry
@@ -508,8 +563,10 @@
             first = col * count + r * chunk
             half = visit_half[rows, 0:1]
             x = seen[v, rows, :]
-            block = panel_rows(x, panel, half, sq_row, first, visit_row, share, panel_extra_ref)
-            seen_high[rows, :], seen_low[rows, :] = split(solved(block, high, low))
+            values = factor_rows(
+                x, panel, half, sq_row, first, visit_row, share, panel_extra_ref, (high, low)
+            )
+            seen_high[rows, :], seen_low[rows, :] = split(values)
 
         @pl.when(v == 0)
         def _():
@@ -649,11 +706,11 @@
     beside = sent(leaving, [(r, r ^ 1) for r in rows])
     across = sent(leaving, [(r, r ^ 2) for r in rows])
 
-    high, low, sq, panel = inverse_lower(place, pieces, panel_extra, share)
+    sq, panel, *state = start_lower(place, pieces, panel_extra, share)
 
     mid = slice_rows // 2
     spot = lax.rem(row_index, LAYER)
-    beside2, across2, above2 = (after(block, high) for block in (beside, across, above))
+    beside2, across2, above2 = (after(block, *state) for block in (beside, across, above))
     up2 = jnp.where(spot == 1, across2[:mid], beside2[mid:])
     x2 = jnp.where(spot == 2, across2[mid:], above2[:mid])
     y2 = jnp.where(spot == 2, above2[:mid], jnp.where(spot == 3, above2[mid:], beside2[:mid]))
@@ -661,14 +718,15 @@
     x2 = sent(x2, [(r, r ^ 1) for r in spots(1, 2, 3)])
     y2 = sent(y2, [(r, r ^ 2) for r in rows])
 
-    trailing, factor, block_high, block_low, half = own_rows(
-        place, slices, panel, high, low, sq, panel_extra, own_extra, share
-    )
-    up2, x2, y2, half = lax.optimization_barrier((up2, x2, y2, half))
+    high, low = finish_lower(state)
+    up2, x2, y2, high = lax.optimization_barrier((up2, x2, y2, high))
     x3 = jnp.where(spot == 1, up2, jnp.where(spot == 0, y2, across2[mid:]))
     up3 = sent(across2[mid:], [(r, up(r)) for r in spots(0)])
     x3 = sent(x3, [(r, r ^ 1) for r in spots(0, 1, 3)])
     y3 = sent(up2, [(r, r ^ 2) for r in spots(2, 3)])
+    trailing, factor, block_high, block_low, half = own_rows(
+        place, slices, panel, high, low, sq, panel_extra, own_extra, share
+    )
     arrivals = {
         "across": across,
         "beside": beside,
@@ -705,8 +763,8 @@
     )
     own = (high, low, sq, block_high, block_low, half)
     rest = (slices, panel, own, panel_extra)
-    trailing = visit("visit_first", (first,), share, place, arrivals, *rest, trailing)
-    trailing = visit("visit_rest", (second, third), share, place, arrivals, *rest, trailing)
+    routes = (first, second, third)
+    trailing = visit("visit_all", routes, share, place, arrivals, *rest, trailing)
     return (trailing, factor)
 
 

time: 205 us -> 217 us (1.059)
  waiting for transfers between devices: 32.8 us -> 43.9 us
    ppermute x15, waiting for transfers between devices: 32.5 us -> 43.6 us  [sent(): return lax.ppermute(block, 'row', pairs)]
    pallas_call x1 -> x2, Pallas kernels: 49.3 us -> 54.2 us  [the longest x1 38.3 us: start_lower(): pl.pallas_call(functools.partial(start_kernel, cols, layers, share), out_...]
    pallas_call x2 -> x1, Pallas kernels: 46.4 us -> 41.5 us  [visit(): pl.pallas_call(functools.partial(visit_kernel, cols, share, routes), out_...]
  transfers between devices with their start and end apart: 21 -> 21, of which waited for: 7 -> 11; matrix products, arithmetic and copies ran while one was open for 6% -> 3% of each run, Pallas kernels for 47% -> 39%
where the time goes in v3:
time: 217 us
  Pallas kernels  127 us (59%)
  waiting for transfers between devices  43.9 us (20%)
  starting transfers between devices  31.1 us (14%)
  other arithmetic  9.36 us (4%)
  local copies, waits for them, and re-layouts  4.73 us (2%)
    ppermute x15, waiting for transfers between devices, sent(): return lax.ppermute(block, 'row', pairs)  43.6 us
    pallas_call x1, Pallas kernels, visit(): pl.pallas_call(functools.partial(visit_kernel, cols, share, routes), out_...  41.5 us
    pallas_call x1, Pallas kernels, start_lower(): pl.pallas_call(functools.partial(start_kernel, cols, layers, share), out_...  38.3 us
    ppermute x15, starting transfers between devices, sent(): return lax.ppermute(block, 'row', pairs)  28.2 us
    pallas_call x1, Pallas kernels, own_rows(): pl.pallas_call(functools.partial(own_kernel, cols, share), out_shape=(jax...  24.4 us
    pallas_call x1, Pallas kernels, finish_lower(): pl.pallas_call(rest_kernel, out_shape=(jax.ShapeDtypeStruct((size, size),...  15.9 us
    pallas_call x1, Pallas kernels, match_extras(): pl.pallas_call(functools.partial(extras_kernel, min(total, 1024)), out_sh...  6.66 us
  transfers between devices with their start and end apart: 21, of which 11 were waited for; matrix products, arithmetic and copies ran while one was open for 3% of the time, Pallas kernels for 39%

profile of v3, /device:TPU:0, one launch (start us, length us, event | category | flops | bytes accessed | tf_op | source)
XLA Modules:
  0.0 216.8 jit_solution(16733608046261616345)
XLA Ops:
  0.6 0.9 slice.30
  1.5 2.4 %collective-permute-start = (bf16[64,1024]{1,0:T(8,128)(2,1)S(1)}, bf16[64,1024]{1,0:T(8,128)(2,1)S(1)}, u32[]{:S(2)}, u32[]{:S(2)}) collective-permute-start(bf16[64,1024]{1,0:T(8,128)(2,1)S(1)} %slice.30), channel_id=1, source_target_pairs={{0,1},{2,3},{4,5},{6,7},{8,9},{10,11},{12,13},{14,15},{16,17},{18,... | collective-permute-start | bytes 393224 | tf_op jit(solution)/shard_map/ppermute | solution.py:680
  3.9 0.7 dynamic_slice.6
  4.6 0.3 collective-permute-done
  4.9 1.0 multiply_convert_fusion.1
  5.8 4.5 %collective-permute-start.3 = (bf16[64,1024]{1,0:T(8,128)(2,1)S(1)}, bf16[64,1024]{1,0:T(8,128)(2,1)S(1)}, u32[]{:S(2)}, u32[]{:S(2)}) collective-permute-start(bf16[64,1024]{1,0:T(8,128)(2,1)S(1)} %multiply_convert_fusion.1), channel_id=1, source_target_pairs={{0,24},{2,26},{4,28},{6,30},{8,0},{10,2},{12,4},{14,6},{16,8},{18,... | collective-permute-start | bytes 393224 | tf_op jit(solution)/shard_map/ppermute | solution.py:652
  10.3 0.0 collective-permute-start.2
  10.3 1.0 collective-permute-start.1
  11.4 2.1 multiply_convert_fusion.refs_0_.refs_8_
  13.5 0.7 collective-permute-done.3
  14.3 8.1 %collective-permute-done.2 = bf16[64,1024]{1,0:T(8,128)(2,1)S(1)} collective-permute-done((bf16[64,1024]{1,0:T(8,128)(2,1)S(1)}, bf16[64,1024]{1,0:T(8,128)(2,1)S(1)}, u32[]{:S(2)}, u32[]{:S(2)}) %collective-permute-start.2) | collective-permute-done | bytes 131104 | tf_op jit(solution)/shard_map/ppermute | solution.py:652
  22.4 0.0 copy-start.6
  22.4 0.1 collective-permute-start.9
  22.5 2.5 %collective-permute-start.6 = (bf16[256,1024]{1,0:T(8,128)(2,1)S(1)}, bf16[256,1024]{1,0:T(8,128)(2,1)}, u32[]{:S(2)}, u32[]{:S(2)}) collective-permute-start(bf16[256,1024]{1,0:T(8,128)(2,1)S(1)} %pad_maximum_fusion.refs_0_), channel_id=1, source_target_pairs={{0,6},{2,4},{4,2},{6,0},{8,14},{10,12},{12,10},{14,8},{16,22},{18,... | collective-permute-start | bytes 1572872 | tf_op jit(solution)/shard_map/ppermute | solution.py:652
  25.0 0.5 collective-permute-start.5
  25.5 0.5 collective-permute-start.4
  26.0 6.7 %match_extras.1 = f32[128,128]{1,0:T(8,128)} custom-call(s32[2,16384]{1,0:T(2,128)} %bitcast.3), custom_call_target="tpu_custom_call" | custom-call | flops 8000000000 | bytes 131072 | tf_op jit(solution)/shard_map/match_extras/pallas_call | solution.py:91
  32.7 5.6 %collective-permute-done.6.refs_3_ = bf16[256,1024]{1,0:T(8,128)(2,1)} collective-permute-done((bf16[256,1024]{1,0:T(8,128)(2,1)S(1)}, bf16[256,1024]{1,0:T(8,128)(2,1)}, u32[]{:S(2)}, u32[]{:S(2)}) %collective-permute-start.6) | collective-permute-done | bytes 524320 | tf_op jit(solution)/shard_map/ppermute | solution.py:652
  38.3 10.7 %collective-permute-done.5.refs_2_ = bf16[256,1024]{1,0:T(8,128)(2,1)} collective-permute-done((bf16[256,1024]{1,0:T(8,128)(2,1)S(1)}, bf16[256,1024]{1,0:T(8,128)(2,1)}, u32[]{:S(2)}, u32[]{:S(2)}) %collective-permute-start.5) | collective-permute-done | bytes 524320 | tf_op jit(solution)/shard_map/ppermute | solution.py:652
  49.0 0.1 collective-permute-done.4.refs_1_
  49.1 0.5 collective-permute-start.11
  49.7 0.0 collective-permute-start.12
  49.7 0.6 pad_add_fusion.place_ref
  50.3 0.9 reshape.12
  51.2 0.7 reshape.13.refs_8_.refs_6_.refs_17_
  51.8 2.0 collective-permute-start.14
  53.8 1.9 collective-permute-start.8
  55.8 0.7 collective-permute-start.7
  56.5 38.3 %start_lower.1 = (f32[8,1024]{1,0:T(8,128)}, bf16[1024,2048]{1,0:T(8,128)(2,1)}, f32[1024,1024]{1,0:T(8,128)}, f32[128,128]{1,0:T(8,128)}, bf16[128,128]{1,0:T(8,128)(2,1)}, /*index=5*/bf16[128,128]{1,0:T(8,128)(2,1)}) custom-call(s32[2]{0:T(128)} %pad_add_fusion.place_ref, bf16[256,1024]{1,0:T(8,128)(2,1)} %copy-done.6, ...), custom_call_target="tpu_custom_call" | custom-call | flops 49999998976 | bytes 8388608 | tf_op jit(solution)/shard_map/start_lower/pallas_call | solution.py:322
  94.8 7.1 %collective-permute-done.8.refs_1_ = bf16[512,2048]{1,0:T(8,128)(2,1)S(1)} collective-permute-done((bf16[512,2048]{1,0:T(8,128)(2,1)S(1)}, bf16[512,2048]{1,0:T(8,128)(2,1)S(1)}, u32[]{:S(2)}, u32[]{:S(2)}) %collective-permute-start.8) | collective-permute-done | bytes 2097184 | tf_op jit(solution)/shard_map/ppermute | solution.py:652
  101.9 1.4 collective-permute-done.7.refs_0_
  103.3 4.1 %select_select_fusion.1 = (bf16[256,2048]{1,0:T(8,128)(2,1)}, bf16[256,2048]{1,0:T(8,128)(2,1)}, bf16[256,2048]{1,0:T(8,128)(2,1)}) fusion(bf16[512,2048]{1,0:T(8,128)(2,1)S(1)} %collective-permute-done.8.refs_1_, bf16[512,2048]{1,0:T(8,128)(2,1)} %collective-permute-done.14, pred[]{:T(512)S(6)} %eq.24, pred[]{:T(512)S(6)} %eq.23, ...), kind=kLoop, calls=%fused_computation.2 | loop fusion | flops 2097152 | bytes 9437187 | tf_op jit(solution)/shard_map/jit(_where)/select_n | solution.py:716
  107.3 2.6 %collective-permute-start.16 = (bf16[256,2048]{1,0:T(8,128)(2,1)}, bf16[256,2048]{1,0:T(8,128)(2,1)S(1)}, u32[]{:S(2)}, u32[]{:S(2)}) collective-permute-start(bf16[256,2048]{1,0:T(8,128)(2,1)} %get-tuple-element.56), channel_id=1, source_target_pairs={{0,4},{2,6},{4,0},{6,2},{8,12},{10,14},{12,8},{14,10},{16,20},{18,... | collective-permute-start | bytes 3145736 | tf_op jit(solution)/shard_map/ppermute | solution.py:652
  110.0 1.3 collective-permute-start.15
  111.3 1.1 collective-permute-start.13
  112.3 15.9 %finish_lower.1 = (bf16[1024,1024]{1,0:T(8,128)(2,1)}, bf16[1024,1024]{1,0:T(8,128)(2,1)}) custom-call(f32[1024,1024]{1,0:T(8,128)} %get-tuple-element.33.work_hbm, f32[128,128]{1,0:T(8,128)} %get-tuple-element.34.ahead_in, bf16[128,128]{1,0:T(8,128)(2,1)} %get-tuple-element.35.inv_high_in, bf16[128,128]{1,0:T(8,128)(2,1)} %get-tuple-element.36.inv_low_in), custom_call_target="tpu_custom_call" | custom-call | flops 1024 | bytes 1024 | tf_op jit(solution)/shard_map/finish_lower/pallas_call | solution.py:249
  128.3 5.0 %collective-permute-done.16.refs_6_ = bf16[256,2048]{1,0:T(8,128)(2,1)S(1)} collective-permute-done((bf16[256,2048]{1,0:T(8,128)(2,1)}, bf16[256,2048]{1,0:T(8,128)(2,1)S(1)}, u32[]{:S(2)}, u32[]{:S(2)}) %collective-permute-start.16) | collective-permute-done | bytes 1048608 | tf_op jit(solution)/shard_map/ppermute | solution.py:652
  133.2 3.4 %collective-permute-done.15.refs_4_ = bf16[256,2048]{1,0:T(8,128)(2,1)} collective-permute-done((bf16[256,2048]{1,0:T(8,128)(2,1)}, bf16[256,2048]{1,0:T(8,128)(2,1)}, u32[]{:S(2)}, u32[]{:S(2)}) %collective-permute-start.15) | collective-permute-done | bytes 1048608 | tf_op jit(solution)/shard_map/ppermute | solution.py:652
  136.7 1.4 collective-permute-done.13.refs_2_
  138.1 1.3 collective-permute-start.19
  139.4 1.5 select_select_fusion
  140.9 6.2 %collective-permute-start.18 = (bf16[256,2048]{1,0:T(8,128)(2,1)}, bf16[256,2048]{1,0:T(8,128)(2,1)S(1)}, u32[]{:S(2)}, u32[]{:S(2)}) collective-permute-start(bf16[256,2048]{1,0:T(8,128)(2,1)} %get-tuple-element.54), channel_id=1, source_target_pairs={{0,2},{2,0},{6,4},{8,10},{10,8},{14,12},{16,18},{18,16},{22,20},{2... | collective-permute-start | bytes 3145736 | tf_op jit(solution)/shard_map/ppermute | solution.py:652
  147.2 1.9 collective-permute-start.17
  149.1 0.6 dynamic_slice.7.refs_7_
  149.7 24.4 %own_rows.1 = (f32[1024,2048]{1,0:T(8,128)}, f32[512,1024]{1,0:T(8,128)}, bf16[1024,1024]{1,0:T(8,128)(2,1)}, bf16[1024,1024]{1,0:T(8,128)(2,1)}, f32[1024,128]{1,0:T(8,128)}) custom-call(s32[2]{0:T(128)} %pad_add_fusion.place_ref, bf16[512,2048]{1,0:T(8,128)(2,1)} %copy-done, bf16[512,2048]{1,0:T(8,128)(2,1)} %collective-permute-done.20.refs_1_.refs_9_, ...), custom_call_target="tpu_custom_call" | custom-call | flops 1048576 | bytes 1048576 | tf_op jit(solution)/shard_map/own_rows/pallas_call | solution.py:454
  174.1 0.0 collective-permute-done.17.refs_3_
  174.2 1.0 copy-done.5
  175.1 41.5 %visit_all.1 = f32[1024,2048]{1,0:T(8,128)} custom-call(s32[2]{0:T(128)} %pad_add_fusion.place_ref, bf16[512,2048]{1,0:T(8,128)(2,1)} %copy-done.1, bf16[512,2048]{1,0:T(8,128)(2,1)} %copy-done.3, bf16[256,2048]{1,0:T(8,128)(2,1)} %collective-permute-done.13.refs_2_, ...), custom_call_target="tpu_custom_call", output_to_operand_aliasing={{}: (19, {})} | custom-call | flops 524288 | bytes 524288 | tf_op jit(solution)/shard_map/visit_all/pallas_call | solution.py:607
  (25 shorter events, 0.1 us)
Async XLA Ops:
  1.5 3.3 %collective-permute-start = (bf16[64,1024]{1,0:T(8,128)(2,1)S(1)}, bf16[64,1024]{1,0:T(8,128)(2,1)S(1)}, u32[]{:S(2)}, u32[]{:S(2)}) collective-permute-start(bf16[64,1024]{1,0:T(8,128)(2,1)S(1)} %slice.30), channel_id=1, source_target_pairs={{0,1},{2,3},{4,5},{6,7},{8,9},{10,11},{12,13},{14,15},{16,17},{18,... | collective-permute-start | bytes 393224 | tf_op jit(solution)/shard_map/ppermute | solution.py:680
  5.8 8.4 %collective-permute-start.3 = (bf16[64,1024]{1,0:T(8,128)(2,1)S(1)}, bf16[64,1024]{1,0:T(8,128)(2,1)S(1)}, u32[]{:S(2)}, u32[]{:S(2)}) collective-permute-start(bf16[64,1024]{1,0:T(8,128)(2,1)S(1)} %multiply_convert_fusion.1), channel_id=1, source_target_pairs={{0,24},{2,26},{4,28},{6,30},{8,0},{10,2},{12,4},{14,6},{16,8},{18,... | collective-permute-start | bytes 393224 | tf_op jit(solution)/shard_map/ppermute | solution.py:652
  10.3 12.0 %collective-permute-start.2 = (bf16[64,1024]{1,0:T(8,128)(2,1)S(1)}, bf16[64,1024]{1,0:T(8,128)(2,1)S(1)}, u32[]{:S(2)}, u32[]{:S(2)}) collective-permute-start(bf16[64,1024]{1,0:T(8,128)(2,1)S(1)} %multiply_convert_fusion.1), channel_id=1, source_target_pairs={{0,16},{2,18},{4,20},{6,22},{8,24},{10,26},{12,28},{14,30},{16,0},... | collective-permute-start | bytes 393224 | tf_op jit(solution)/shard_map/ppermute | solution.py:652
  10.3 12.0 %collective-permute-start.1 = (bf16[64,1024]{1,0:T(8,128)(2,1)S(1)}, bf16[64,1024]{1,0:T(8,128)(2,1)S(1)}, u32[]{:S(2)}, u32[]{:S(2)}) collective-permute-start(bf16[64,1024]{1,0:T(8,128)(2,1)S(1)} %multiply_convert_fusion.1), channel_id=1, source_target_pairs={{0,8},{2,10},{4,12},{6,14},{8,16},{10,18},{12,20},{14,22},{16,24},... | collective-permute-start | bytes 393224 | tf_op jit(solution)/shard_map/ppermute | solution.py:652
  13.5 98.8 %copy-start = (bf16[512,2048]{1,0:T(8,128)(2,1)}, bf16[512,2048]{1,0:T(8,128)(2,1)S(1)}, u32[]{:S(2)}) copy-start(bf16[512,2048]{1,0:T(8,128)(2,1)S(1)} %multiply_convert_fusion.refs_0_.refs_8_) | copy-start | bytes 6291460
  22.4 10.3 %copy-start.6 = (bf16[256,1024]{1,0:T(8,128)(2,1)}, bf16[256,1024]{1,0:T(8,128)(2,1)S(1)}, u32[]{:S(2)}) copy-start(bf16[256,1024]{1,0:T(8,128)(2,1)S(1)} %pad_maximum_fusion.refs_0_) | copy-start | bytes 1572868
  22.4 31.5 %collective-permute-start.9 = (bf16[256,1024]{1,0:T(8,128)(2,1)S(1)}, bf16[256,1024]{1,0:T(8,128)(2,1)}, u32[]{:S(2)}, u32[]{:S(2)}) collective-permute-start(bf16[256,1024]{1,0:T(8,128)(2,1)S(1)} %pad_maximum_fusion.refs_0_), channel_id=1, source_target_pairs={{0,1},{1,0},{2,3},{3,2},{4,5},{5,4},{6,7},{7,6},{8,9},{9,8},{10,11... | collective-permute-start | bytes 1572872 | tf_op jit(solution)/shard_map/ppermute | solution.py:27
  22.5 15.8 %collective-permute-start.6 = (bf16[256,1024]{1,0:T(8,128)(2,1)S(1)}, bf16[256,1024]{1,0:T(8,128)(2,1)}, u32[]{:S(2)}, u32[]{:S(2)}) collective-permute-start(bf16[256,1024]{1,0:T(8,128)(2,1)S(1)} %pad_maximum_fusion.refs_0_), channel_id=1, source_target_pairs={{0,6},{2,4},{4,2},{6,0},{8,14},{10,12},{12,10},{14,8},{16,22},{18,... | collective-permute-start | bytes 1572872 | tf_op jit(solution)/shard_map/ppermute | solution.py:652
  25.0 24.1 %collective-permute-start.5 = (bf16[256,1024]{1,0:T(8,128)(2,1)S(1)}, bf16[256,1024]{1,0:T(8,128)(2,1)}, u32[]{:S(2)}, u32[]{:S(2)}) collective-permute-start(bf16[256,1024]{1,0:T(8,128)(2,1)S(1)} %pad_maximum_fusion.refs_0_), channel_id=1, source_target_pairs={{0,4},{2,6},{4,0},{6,2},{8,12},{10,14},{12,8},{14,10},{16,20},{18,... | collective-permute-start | bytes 1572872 | tf_op jit(solution)/shard_map/ppermute | solution.py:652
  25.5 23.7 %collective-permute-start.4 = (bf16[256,1024]{1,0:T(8,128)(2,1)S(1)}, bf16[256,1024]{1,0:T(8,128)(2,1)}, u32[]{:S(2)}, u32[]{:S(2)}) collective-permute-start(bf16[256,1024]{1,0:T(8,128)(2,1)S(1)} %pad_maximum_fusion.refs_0_), channel_id=1, source_target_pairs={{0,2},{2,0},{4,6},{6,4},{8,10},{10,8},{12,14},{14,12},{16,18},{18,... | collective-permute-start | bytes 1572872 | tf_op jit(solution)/shard_map/ppermute | solution.py:652
  49.1 6.6 %collective-permute-start.10 = (bf16[256,1024]{1,0:T(8,128)(2,1)}, bf16[256,1024]{1,0:T(8,128)(2,1)}, u32[]{:S(2)}, u32[]{:S(2)}) collective-permute-start(bf16[256,1024]{1,0:T(8,128)(2,1)} %collective-permute-done.4.refs_1_), channel_id=1, source_target_pairs={{0,1},{1,0},{2,3},{3,2},{4,5},{5,4},{6,7},{7,6},{8,9},{9,8},{10,11... | collective-permute-start | bytes 1572872 | tf_op jit(solution)/shard_map/ppermute | solution.py:27
  49.1 7.4 %collective-permute-start.11 = (bf16[256,1024]{1,0:T(8,128)(2,1)}, bf16[256,1024]{1,0:T(8,128)(2,1)}, u32[]{:S(2)}, u32[]{:S(2)}) collective-permute-start(bf16[256,1024]{1,0:T(8,128)(2,1)} %collective-permute-done.5.refs_2_), channel_id=1, source_target_pairs={{0,1},{1,0},{2,3},{3,2},{4,5},{5,4},{6,7},{7,6},{8,9},{9,8},{10,11... | collective-permute-start | bytes 1572872 | tf_op jit(solution)/shard_map/ppermute | solution.py:27
  49.7 6.9 %collective-permute-start.12 = (bf16[256,1024]{1,0:T(8,128)(2,1)}, bf16[256,1024]{1,0:T(8,128)(2,1)}, u32[]{:S(2)}, u32[]{:S(2)}) collective-permute-start(bf16[256,1024]{1,0:T(8,128)(2,1)} %collective-permute-done.6.refs_3_), channel_id=1, source_target_pairs={{0,1},{1,0},{2,3},{3,2},{4,5},{5,4},{6,7},{7,6},{8,9},{9,8},{10,11... | collective-permute-start | bytes 1572872 | tf_op jit(solution)/shard_map/ppermute | solution.py:27
  51.8 43.0 %collective-permute-start.14 = (bf16[512,2048]{1,0:T(8,128)(2,1)S(1)}, bf16[512,2048]{1,0:T(8,128)(2,1)}, u32[]{:S(2)}, u32[]{:S(2)}) collective-permute-start(bf16[512,2048]{1,0:T(8,128)(2,1)S(1)} %multiply_convert_fusion.refs_0_.refs_8_), channel_id=1, source_target_pairs={{2,10},{4,12},{6,14},{10,18},{12,20},{14,22},{18,26},{20,28},{22,3... | collective-permute-start | bytes 6291464 | tf_op jit(solution)/shard_map/ppermute | solution.py:652
  53.8 48.0 %collective-permute-start.8 = (bf16[512,2048]{1,0:T(8,128)(2,1)S(1)}, bf16[512,2048]{1,0:T(8,128)(2,1)S(1)}, u32[]{:S(2)}, u32[]{:S(2)}) collective-permute-start(bf16[512,2048]{1,0:T(8,128)(2,1)S(1)} %multiply_convert_fusion.refs_0_.refs_8_), channel_id=1, source_target_pairs={{0,2},{2,0},{4,6},{6,4},{8,10},{10,8},{12,14},{14,12},{16,18},{18,... | collective-permute-start | bytes 6291464 | tf_op jit(solution)/shard_map/ppermute | solution.py:652
  55.8 47.5 %collective-permute-start.7 = (bf16[512,2048]{1,0:T(8,128)(2,1)S(1)}, bf16[512,2048]{1,0:T(8,128)(2,1)S(1)}, u32[]{:S(2)}, u32[]{:S(2)}) collective-permute-start(bf16[512,2048]{1,0:T(8,128)(2,1)S(1)} %multiply_convert_fusion.refs_0_.refs_8_), channel_id=1, source_target_pairs={{0,4},{2,6},{4,0},{6,2},{8,12},{10,14},{12,8},{14,10},{16,20},{18,... | collective-permute-start | bytes 6291464 | tf_op jit(solution)/shard_map/ppermute | solution.py:652
  101.9 5.4 %copy-start.3 = (bf16[512,2048]{1,0:T(8,128)(2,1)}, bf16[512,2048]{1,0:T(8,128)(2,1)S(1)}, u32[]{:S(2)}) copy-start(bf16[512,2048]{1,0:T(8,128)(2,1)S(1)} %collective-permute-done.8.refs_1_) | copy-start | bytes 6291460
  103.3 4.1 %copy-start.1 = (bf16[512,2048]{1,0:T(8,128)(2,1)}, bf16[512,2048]{1,0:T(8,128)(2,1)S(1)}, u32[]{:S(2)}) copy-start(bf16[512,2048]{1,0:T(8,128)(2,1)S(1)} %collective-permute-done.7.refs_0_) | copy-start | bytes 6291460
  107.3 25.9 %collective-permute-start.16 = (bf16[256,2048]{1,0:T(8,128)(2,1)}, bf16[256,2048]{1,0:T(8,128)(2,1)S(1)}, u32[]{:S(2)}, u32[]{:S(2)}) collective-permute-start(bf16[256,2048]{1,0:T(8,128)(2,1)} %get-tuple-element.56), channel_id=1, source_target_pairs={{0,4},{2,6},{4,0},{6,2},{8,12},{10,14},{12,8},{14,10},{16,20},{18,... | collective-permute-start | bytes 3145736 | tf_op jit(solution)/shard_map/ppermute | solution.py:652
  110.0 26.7 %collective-permute-start.15 = (bf16[256,2048]{1,0:T(8,128)(2,1)}, bf16[256,2048]{1,0:T(8,128)(2,1)}, u32[]{:S(2)}, u32[]{:S(2)}) collective-permute-start(bf16[256,2048]{1,0:T(8,128)(2,1)} %get-tuple-element.57), channel_id=1, source_target_pairs={{2,0},{4,6},{6,4},{10,8},{12,14},{14,12},{18,16},{20,22},{22,20},{... | collective-permute-start | bytes 3145736 | tf_op jit(solution)/shard_map/ppermute | solution.py:652
  111.3 26.8 %collective-permute-start.13 = (bf16[256,2048]{1,0:T(8,128)(2,1)}, bf16[256,2048]{1,0:T(8,128)(2,1)}, u32[]{:S(2)}, u32[]{:S(2)}) collective-permute-start(bf16[256,2048]{1,0:T(8,128)(2,1)} %get-tuple-element.58), channel_id=1, source_target_pairs={{0,8},{2,10},{4,12},{6,14},{8,16},{10,18},{12,20},{14,22},{16,24},... | collective-permute-start | bytes 3145736 | tf_op jit(solution)/shard_map/ppermute | solution.py:652
  112.3 37.4 %collective-permute-start.20 = (bf16[512,2048]{1,0:T(8,128)(2,1)S(1)}, bf16[512,2048]{1,0:T(8,128)(2,1)}, u32[]{:S(2)}, u32[]{:S(2)}) collective-permute-start(bf16[512,2048]{1,0:T(8,128)(2,1)S(1)} %multiply_convert_fusion.refs_0_.refs_8_), channel_id=1, source_target_pairs={{0,1},{1,0},{2,3},{3,2},{4,5},{5,4},{6,7},{7,6},{8,9},{9,8},{10,11... | collective-permute-start | bytes 6291464 | tf_op jit(solution)/shard_map/ppermute | solution.py:27
  112.3 27.0 %copy-start.2 = (bf16[512,2048]{1,0:T(8,128)(2,1)S(1)}, bf16[512,2048]{1,0:T(8,128)(2,1)}, u32[]{:S(2)}) copy-start(bf16[512,2048]{1,0:T(8,128)(2,1)} %copy-done.1) | copy-start | bytes 6291460
  133.2 7.7 %copy-start.4 = (bf16[256,2048]{1,0:T(8,128)(2,1)}, bf16[256,2048]{1,0:T(8,128)(2,1)S(1)}, u32[]{:S(2)}) copy-start(bf16[256,2048]{1,0:T(8,128)(2,1)S(1)} %collective-permute-done.16.refs_6_) | copy-start | bytes 3145732
  138.1 36.0 %collective-permute-start.19 = (bf16[256,2048]{1,0:T(8,128)(2,1)}, bf16[256,2048]{1,0:T(8,128)(2,1)}, u32[]{:S(2)}, u32[]{:S(2)}) collective-permute-start(bf16[256,2048]{1,0:T(8,128)(2,1)} %collective-permute-done.13.refs_2_), channel_id=1, source_target_pairs={{4,0},{6,2},{12,8},{14,10},{20,16},{22,18},{28,24},{30,26},{5,1},{... | collective-permute-start | bytes 3145736 | tf_op jit(solution)/shard_map/ppermute | solution.py:652
  140.9 33.2 %collective-permute-start.18 = (bf16[256,2048]{1,0:T(8,128)(2,1)}, bf16[256,2048]{1,0:T(8,128)(2,1)S(1)}, u32[]{:S(2)}, u32[]{:S(2)}) collective-permute-start(bf16[256,2048]{1,0:T(8,128)(2,1)} %get-tuple-element.54), channel_id=1, source_target_pairs={{0,2},{2,0},{6,4},{8,10},{10,8},{14,12},{16,18},{18,16},{22,20},{2... | collective-permute-start | bytes 3145736 | tf_op jit(solution)/shard_map/ppermute | solution.py:652
  147.2 27.0 %collective-permute-start.17 = (bf16[256,2048]{1,0:T(8,128)(2,1)}, bf16[256,2048]{1,0:T(8,128)(2,1)}, u32[]{:S(2)}, u32[]{:S(2)}) collective-permute-start(bf16[256,2048]{1,0:T(8,128)(2,1)} %get-tuple-element.55), channel_id=1, source_target_pairs={{0,8},{8,16},{16,24},{24,0},{1,9},{9,17},{17,25},{25,1}} | collective-permute-start | bytes 3145736 | tf_op jit(solution)/shard_map/ppermute | solution.py:652
  174.1 1.0 copy-start.5
